TPU v7x, 128 devices: a whole 4x4x4 slice. The times are simulated.
128 devices in a mesh: band: 4 (over x), set: 32 (over y, z, core).
Axes of the slice: x: 4, y: 4, z: 4, core: 2. Of those that a mesh axis runs over, the one named last changes fastest.
Arguments:
- fields: bfloat16 [2560, 16, 5120], P(('band', 'set')), may hold values from -6 to 6
- depart: int32 [2560, 40, 4], P(('band', 'set')), may hold values from 0 to 102399, as said below
- blend: float32 [2560, 40, 4, 128], P(('band', 'set')), may hold values from 0.05 to 0.45
- wave_owner: int32 [1280], replicated, may hold values from 0 to 1279, each once
- damping: float32 [16], replicated, may hold values from 0.5 to 8
Outputs:
- updated: bfloat16 [2560, 16, 5120], P(('band', 'set'))
- spectra: float32 [1280, 16, 2, 1280], P(('band', 'set'))
Inputs may be any that keep to these rules, and one draw needn't show every extreme that they name: The cycle depart[r, b, k] // 40 lies within 4 cycles of r; on every device some entry lies exactly 4 cycles away. `wave_owner`: each zonal wavenumber appears exactly once.
All inputs are finite; a program needn't handle non-finite values.
Results may differ from a plain program's by a relative error of at most 0.0077.
Values may be sent and summed in bfloat16 or wider, within the bound.
A program may use at most 192 MiB of HBM per device.

v0:
```python
import math

import jax
import jax.numpy as jnp
from jax import lax
from jax.sharding import PartitionSpec as P

NLAT = 2560
NLON = 5120
MM = 1280
LEV = 8
BW = 128
K = 4
HALO = 4
NBK = 128
XB = 512
FL = 16
NB = 40


def with_halo(block, sides, width):
    for axis, dim in sides:
        count = lax.axis_size(axis)
        forward = [(i, i + 1) for i in range(count - 1)]
        backward = [(target, source) for source, target in forward]
        low = lax.ppermute(
            lax.slice_in_dim(block, block.shape[dim] - width, None, axis=dim), axis, forward
        )
        high = lax.ppermute(lax.slice_in_dim(block, 0, width, axis=dim), axis, backward)
        block = jnp.concatenate([low, block, high], axis=dim)
    return block


def forward_table(columns, wavenums):
    index_mod = columns[:, None] * wavenums[None, :] % NLON
    angles = index_mod.astype(jnp.float32) * (2.0 * math.pi / NLON)
    norm_scale = math.sqrt(2.0 / NLON)
    stacked = jnp.stack([norm_scale * jnp.cos(angles), -norm_scale * jnp.sin(angles)], axis=1)
    return stacked.reshape(columns.shape[0], 2 * wavenums.shape[0]).astype(jnp.bfloat16)


def backward_table(columns, wavenums):
    index_mod = wavenums[:, None] * columns[None, :] % NLON
    angles = index_mod.astype(jnp.float32) * (2.0 * math.pi / NLON)
    weight = jnp.where(wavenums == 0, 0.5, 1.0).astype(jnp.float32) * math.sqrt(2.0 / NLON)
    stacked = jnp.stack(
        [weight[:, None] * jnp.cos(angles), -weight[:, None] * jnp.sin(angles)], axis=0
    )
    return stacked.reshape(2 * wavenums.shape[0], columns.shape[0]).astype(jnp.bfloat16)


def basis_rows(count):
    orders = jnp.arange(count, dtype=jnp.int32)
    lat_index = jnp.arange(NLAT, dtype=jnp.int32)
    index_mod = orders[:, None] * (2 * lat_index[None, :] + 1) % (4 * NLAT)
    angles = index_mod.astype(jnp.float32) * (math.pi / (2 * NLAT))
    norm_scale = jnp.where(orders == 0, math.sqrt(1.0 / NLAT), math.sqrt(2.0 / NLAT)).astype(
        jnp.float32
    )
    return norm_scale[:, None] * jnp.cos(angles)


def damping_factors(damping):
    orders = jnp.arange(MM, dtype=jnp.int32).astype(jnp.float32)
    ratio = orders * (orders + 1.0) / (MM * (MM - 1.0))
    level_ids = jnp.arange(damping.shape[0], dtype=jnp.int32)
    powered = jnp.where(level_ids[:, None] < LEV, ratio[None, :] * ratio[None, :], ratio[None, :])
    return 1.0 / (1.0 + damping[:, None] * powered)


def per_device(fields, depart, blend, wave_owner, damping):
    lat_dev = fields.shape[0]
    band_count = lax.axis_size("band")
    set_count = lax.axis_size("set")
    m_dev = MM // (band_count * set_count)
    device = lax.axis_index(("band", "set"))
    highest = lax.Precision.HIGHEST
    padded = with_halo(fields, ((("band", "set"), 0),), HALO)
    grid_view = padded.reshape(lat_dev + 2 * HALO, FL, NB, BW)
    src_cycle = depart // NB - (device * lat_dev - HALO)
    src_block = depart % NB
    summed = jnp.zeros((lat_dev, NB, FL, BW), jnp.float32)
    for k in range(K):
        gathered = grid_view[src_cycle[:, :, k], :, src_block[:, :, k], :]
        summed = summed + blend[:, :, k, None, :] * gathered.astype(jnp.float32)
    departed = summed.transpose(0, 2, 1, 3).reshape(lat_dev, FL, NLON).astype(jnp.bfloat16)
    grid_rows = departed.reshape(lat_dev * FL, NLON)

    def add_lon(step, running):
        first = step * XB
        segment = lax.dynamic_slice_in_dim(grid_rows, first, XB, 1)
        cosines = forward_table(first + jnp.arange(XB, dtype=jnp.int32), wave_owner)
        return running + jnp.dot(segment, cosines, preferred_element_type=jnp.float32)

    coeffs = lax.fori_loop(0, NLON // XB, add_lon, jnp.zeros((lat_dev * FL, 2 * MM), jnp.float32))
    fourier = coeffs.astype(jnp.bfloat16).reshape(lat_dev, 2 * FL, MM)
    waves_here = lax.all_to_all(fourier, ("band", "set"), split_axis=2, concat_axis=0, tiled=True)
    waves_f = waves_here.astype(jnp.float32)
    owned = lax.dynamic_slice_in_dim(wave_owner, device * m_dev, m_dev, 0)
    orders = jnp.arange(MM, dtype=jnp.int32)
    keep_mask = (orders[None, :] >= owned[:, None]).astype(jnp.float32)
    factors = damping_factors(damping)
    basis = basis_rows(MM)
    first_block = jnp.int32(0)

    def fwd_block(step, running):
        first = step * NBK
        rows_here = lax.dynamic_slice_in_dim(basis, first, NBK, 0)
        values = jnp.einsum("jcm,nj->mcn", waves_f, rows_here, precision=highest)
        return lax.dynamic_update_slice(running, values, (0, 0, first))

    raw_spectra = lax.fori_loop(
        first_block, MM // NBK, fwd_block, jnp.zeros((m_dev, 2 * FL, MM), jnp.float32)
    )
    spectra = (
        raw_spectra.reshape(m_dev, FL, 2, MM)
        * factors[None, :, None, :]
        * keep_mask[:, None, None, :]
    )
    flat_spectra = spectra.reshape(m_dev, 2 * FL, MM)

    def add_block(step, running):
        first = step * NBK
        segment = lax.dynamic_slice_in_dim(flat_spectra, first, NBK, 2)
        rows_here = lax.dynamic_slice_in_dim(basis, first, NBK, 0)
        return running + jnp.einsum("mcn,nj->jcm", segment, rows_here, precision=highest)

    zonal_f = lax.fori_loop(
        first_block, MM // NBK, add_block, jnp.zeros((NLAT, 2 * FL, m_dev), jnp.float32)
    )
    zonal = zonal_f.astype(jnp.bfloat16)
    cycles_here = lax.all_to_all(zonal, ("band", "set"), split_axis=0, concat_axis=2, tiled=True)
    zonal_rows = cycles_here.reshape(lat_dev * FL, 2 * MM)

    def put_lon(step, result):
        first = step * XB
        cosines = backward_table(first + jnp.arange(XB, dtype=jnp.int32), wave_owner)
        values = jnp.dot(zonal_rows, cosines, preferred_element_type=jnp.float32).astype(
            jnp.bfloat16
        )
        return lax.dynamic_update_slice(result, values, (0, first))

    result = lax.fori_loop(0, NLON // XB, put_lon, jnp.zeros((lat_dev * FL, NLON), jnp.bfloat16))
    updated = result.reshape(lat_dev, FL, NLON)
    return (updated, spectra)


def solution(mesh):
    in_specs = (
        P(("band", "set"), None, None),
        P(("band", "set"), None, None),
        P(("band", "set"), None, None, None),
        P(),
        P(),
    )
    out_specs = (P(("band", "set"), None, None), P(("band", "set"), None, None, None))
    return jax.shard_map(
        per_device, mesh=mesh, in_specs=in_specs, out_specs=out_specs, check_vma=False
    )
```

profile of v0, /device:TPU:1, one launch (start us, length us, event | category | flops | bytes accessed | tf_op | source)
XLA Modules:
  0.0 792.7 jit_solution(5082198505665646986)
XLA Ops:
  11.5 6.1 fusion.73
  24.6 9.5 %gather_fusion = bf16[800,16,128]{2,1,0:T(8,128)(2,1)} fusion(bf16[28,16,40,128]{3,1,2,0:T(8,128)(2,1)} %copy_bitcast_fusion, s32[800]{0:T(1024)S(1)} %reshape.458), kind=kCustom, calls=%fused_computation | custom fusion | bytes 6560000 | tf_op jit(solution)/shard_map/gather | solution.py:84
  34.0 9.5 %gather_fusion.1 = bf16[800,16,128]{2,1,0:T(8,128)(2,1)} fusion(bf16[28,16,40,128]{3,1,2,0:T(8,128)(2,1)} %copy_bitcast_fusion, s32[800]{0:T(1024)S(1)} %reshape.464), kind=kCustom, calls=%fused_computation.1 | custom fusion | bytes 6560000 | tf_op jit(solution)/shard_map/gather | solution.py:84
  43.5 9.8 %gather_fusion.2 = bf16[800,16,128]{2,1,0:T(8,128)(2,1)} fusion(bf16[28,16,40,128]{3,1,2,0:T(8,128)(2,1)} %copy_bitcast_fusion, s32[800]{0:T(1024)S(1)} %reshape.470), kind=kCustom, calls=%fused_computation.2 | custom fusion | bytes 6560000 | tf_op jit(solution)/shard_map/gather | solution.py:84
  53.4 9.4 %gather_fusion.3 = bf16[800,16,128]{2,1,0:T(8,128)(2,1)} fusion(bf16[28,16,40,128]{3,1,2,0:T(8,128)(2,1)} %copy_bitcast_fusion, s32[800]{0:T(1024)S(1)} %reshape.476), kind=kCustom, calls=%fused_computation.3 | custom fusion | bytes 6560000 | tf_op jit(solution)/shard_map/gather | solution.py:84
  62.8 6.5 fusion.41
  72.5 169.4 %while.54 = (s32[]{:T(128)}, f32[320,2560]{1,0:T(8,128)S(1)}, bf16[320,5120]{1,0:T(8,128)(2,1)}, s32[1280]{0:T(1024)S(1)}, s32[]{:T(128)}, /*index=5*/s32[]{:T(128)}, s32[]{:T(128)}, s32[]{:T(128)}) while((s32[]{:T(128)}, f32[320,2560]{1,0:T(8,128)S(1)}, bf16[320,5120]{1,0:T(8,128)(2,1)}, s32[1280]{0:T(1024)S(1)}, s32[]{:T(128)}, ...), condition=%wide.region_1.2_spmd.clone, body=%wide.region_0.1_spmd.clone.sunk | while | flops 850330112 | bytes 17376404 | solution.py:95
  72.7 11.7 %multiply_convert_fusion.7 = (bf16[512,1,1280]{0,2,1:T(8,128)(2,1)S(1)}, bf16[512,1,1280]{0,2,1:T(8,128)(2,1)S(1)}) fusion(s32[1280]{0:T(1024)S(1)} %get-tuple-element.485, s32[512]{0:T(512)S(1)} %iota_add_fusion.5), kind=kLoop, calls=%fused_computation.32.clone.1 | loop fusion | flops 8519680 | bytes 2628608 | tf_op jit(solution)/shard_map/convert
  89.6 11.7 %multiply_convert_fusion.7 = (bf16[512,1,1280]{0,2,1:T(8,128)(2,1)S(1)}, bf16[512,1,1280]{0,2,1:T(8,128)(2,1)S(1)}) fusion(s32[1280]{0:T(1024)S(1)} %get-tuple-element.485, s32[512]{0:T(512)S(1)} %iota_add_fusion.5), kind=kLoop, calls=%fused_computation.32.clone.1 | loop fusion | flops 8519680 | bytes 2628608 | tf_op jit(solution)/shard_map/convert
  106.6 11.7 %multiply_convert_fusion.7 = (bf16[512,1,1280]{0,2,1:T(8,128)(2,1)S(1)}, bf16[512,1,1280]{0,2,1:T(8,128)(2,1)S(1)}) fusion(s32[1280]{0:T(1024)S(1)} %get-tuple-element.485, s32[512]{0:T(512)S(1)} %iota_add_fusion.5), kind=kLoop, calls=%fused_computation.32.clone.1 | loop fusion | flops 8519680 | bytes 2628608 | tf_op jit(solution)/shard_map/convert
  123.5 11.7 %multiply_convert_fusion.7 = (bf16[512,1,1280]{0,2,1:T(8,128)(2,1)S(1)}, bf16[512,1,1280]{0,2,1:T(8,128)(2,1)S(1)}) fusion(s32[1280]{0:T(1024)S(1)} %get-tuple-element.485, s32[512]{0:T(512)S(1)} %iota_add_fusion.5), kind=kLoop, calls=%fused_computation.32.clone.1 | loop fusion | flops 8519680 | bytes 2628608 | tf_op jit(solution)/shard_map/convert
  140.4 11.7 %multiply_convert_fusion.7 = (bf16[512,1,1280]{0,2,1:T(8,128)(2,1)S(1)}, bf16[512,1,1280]{0,2,1:T(8,128)(2,1)S(1)}) fusion(s32[1280]{0:T(1024)S(1)} %get-tuple-element.485, s32[512]{0:T(512)S(1)} %iota_add_fusion.5), kind=kLoop, calls=%fused_computation.32.clone.1 | loop fusion | flops 8519680 | bytes 2628608 | tf_op jit(solution)/shard_map/convert
  157.3 11.7 %multiply_convert_fusion.7 = (bf16[512,1,1280]{0,2,1:T(8,128)(2,1)S(1)}, bf16[512,1,1280]{0,2,1:T(8,128)(2,1)S(1)}) fusion(s32[1280]{0:T(1024)S(1)} %get-tuple-element.485, s32[512]{0:T(512)S(1)} %iota_add_fusion.5), kind=kLoop, calls=%fused_computation.32.clone.1 | loop fusion | flops 8519680 | bytes 2628608 | tf_op jit(solution)/shard_map/convert
  174.3 11.7 %multiply_convert_fusion.7 = (bf16[512,1,1280]{0,2,1:T(8,128)(2,1)S(1)}, bf16[512,1,1280]{0,2,1:T(8,128)(2,1)S(1)}) fusion(s32[1280]{0:T(1024)S(1)} %get-tuple-element.485, s32[512]{0:T(512)S(1)} %iota_add_fusion.5), kind=kLoop, calls=%fused_computation.32.clone.1 | loop fusion | flops 8519680 | bytes 2628608 | tf_op jit(solution)/shard_map/convert
  191.2 11.7 %multiply_convert_fusion.7 = (bf16[512,1,1280]{0,2,1:T(8,128)(2,1)S(1)}, bf16[512,1,1280]{0,2,1:T(8,128)(2,1)S(1)}) fusion(s32[1280]{0:T(1024)S(1)} %get-tuple-element.485, s32[512]{0:T(512)S(1)} %iota_add_fusion.5), kind=kLoop, calls=%fused_computation.32.clone.1 | loop fusion | flops 8519680 | bytes 2628608 | tf_op jit(solution)/shard_map/convert
  208.1 11.7 %multiply_convert_fusion.7 = (bf16[512,1,1280]{0,2,1:T(8,128)(2,1)S(1)}, bf16[512,1,1280]{0,2,1:T(8,128)(2,1)S(1)}) fusion(s32[1280]{0:T(1024)S(1)} %get-tuple-element.485, s32[512]{0:T(512)S(1)} %iota_add_fusion.5), kind=kLoop, calls=%fused_computation.32.clone.1 | loop fusion | flops 8519680 | bytes 2628608 | tf_op jit(solution)/shard_map/convert
  225.0 11.7 %multiply_convert_fusion.7 = (bf16[512,1,1280]{0,2,1:T(8,128)(2,1)S(1)}, bf16[512,1,1280]{0,2,1:T(8,128)(2,1)S(1)}) fusion(s32[1280]{0:T(1024)S(1)} %get-tuple-element.485, s32[512]{0:T(512)S(1)} %iota_add_fusion.5), kind=kLoop, calls=%fused_computation.32.clone.1 | loop fusion | flops 8519680 | bytes 2628608 | tf_op jit(solution)/shard_map/convert
  245.8 10.3 %copy.58 = bf16[20,32,1280]{1,0,2:T(8,128)(2,1)} copy(bf16[20,32,1280]{2,1,0:T(8,128)(2,1)S(1)} %reshape.452) | data formatting | bytes 3276800 | tf_op jit(solution)/shard_map/reshape | solution.py:96
  256.1 11.2 %reshape.492 = bf16[128,2,3200]{2,1,0:T(2,128)(2,1)} reshape(bf16[1280,20,32]{2,1,0:T(8,128)(2,1)} %bitcast.97) | data formatting | bytes 3276800
  267.3 11.9 %all-to-all-start = ((bf16[128,2,3200]{2,1,0:T(2,128)(2,1)}), bf16[128,2,3200]{2,1,0:T(2,128)(2,1)S(1)}, u32[]{:S(2)}, u32[]{:S(2)}) async-start(bf16[128,2,3200]{2,1,0:T(2,128)(2,1)} %reshape.492), calls=%async_computation | async-start | bytes 3276800 | tf_op jit(solution)/shard_map/all_to_all | solution.py:97
  279.2 50.5 %fusion.33 = f32[1280,2560]{1,0:T(8,128)} fusion(s32[2560]{0:T(1024)S(1)} %multiply_add_fusion, f32[1280]{0:T(1024)S(1)} %fusion.70), kind=kLoop, calls=%fused_computation.51 | loop fusion | flops 32768000 | bytes 13122560 | tf_op jit(solution)/shard_map/mul | solution.py:60
  329.7 7.9 reshape.493
  337.5 9.9 %convert_bitcast_fusion = f32[128,20,32,10]{2,1,3,0:T(8,128)} fusion(bf16[20,32,128,10]{1,0,3,2:T(8,128)(2,1)} %bitcast.98), kind=kLoop, calls=%fused_computation.47 | loop fusion | flops 819200 | bytes 4915200 | tf_op jit(solution)/shard_map/convert_element_type | solution.py:98
  347.4 20.3 %copy.59 = f32[128,20,32,10]{1,0,2,3:T(8,128)} copy(f32[128,20,32,10]{2,1,3,0:T(8,128)} %convert_bitcast_fusion) | data formatting | bytes 6553600 | tf_op jit(solution)/shard_map/convert_element_type | solution.py:98
  367.7 18.3 %reshape.456 = f32[2560,32,10]{0,1,2:T(8,128)S(1)} reshape(f32[128,20,32,10]{1,0,2,3:T(8,128)} %copy.59) | data formatting | bytes 6553600 | tf_op jit(solution)/shard_map/convert_element_type | solution.py:98
  387.4 46.9 %while.52 = (s32[]{:T(128)}, f32[10,32,1280]{2,1,0:T(8,128)}, f32[1280,2560]{1,0:T(8,128)}, f32[2560,32,10]{0,1,2:T(8,128)S(1)}, s32[]{:T(128)}, /*index=5*/s32[]{:T(128)}, s32[]{:T(128)}, s32[]{:T(128)}) while((s32[]{:T(128)}, f32[10,32,1280]{2,1,0:T(8,128)}, f32[1280,2560]{1,0:T(8,128)}, f32[2560,32,10]{0,1,2:T(8,128)S(1)}, s32[]{:T(128)}, ...), condition=%wide.region_3.4_spmd, body=%wide.region_2.3_spmd.sunk | while | flops 1258291200 | bytes 4752515 | solution.py:112
  437.2 57.1 %while.55 = (s32[]{:T(128)}, f32[2560,32,10]{0,1,2:T(8,128)S(1)}, f32[1280,2560]{1,0:T(8,128)}, f32[10,32,1280]{2,1,0:T(8,128)}, s32[]{:T(128)}, /*index=5*/s32[]{:T(128)}, s32[]{:T(128)}, s32[]{:T(128)}) while((s32[]{:T(128)}, f32[2560,32,10]{0,1,2:T(8,128)S(1)}, f32[1280,2560]{1,0:T(8,128)}, f32[10,32,1280]{2,1,0:T(8,128)}, ...), condition=%wide.region_5.6_spmd.clone, body=%wide.region_4.5_spmd.clone.sunk | while | flops 1259929600 | bytes 8029836 | solution.py:128
  454.5 5.7 fusion.99
  471.5 5.7 fusion.99
  488.6 5.7 fusion.99
  495.6 11.8 %copy.60 = bf16[2560,32,10]{1,2,0:T(8,128)(2,1)} copy(bf16[2560,32,10]{0,1,2:T(8,128)(2,1)} %convert_element_type.168) | data formatting | bytes 3276800 | tf_op jit(solution)/shard_map/convert_element_type | solution.py:131
  507.4 13.3 %reshape.494 = bf16[128,2,3200]{2,1,0:T(2,128)(2,1)} reshape(bf16[2560,10,32]{2,1,0:T(8,128)(2,1)} %bitcast.95) | data formatting | bytes 3276800
  520.7 10.7 %all-to-all-start.1 = ((bf16[128,2,3200]{2,1,0:T(2,128)(2,1)}), bf16[128,2,3200]{2,1,0:T(2,128)(2,1)}, u32[]{:S(2)}, u32[]{:S(2)}) async-start(bf16[128,2,3200]{2,1,0:T(2,128)(2,1)} %reshape.494), calls=%async_computation.1 | async-start | bytes 3276800 | tf_op jit(solution)/shard_map/all_to_all | solution.py:132
  534.3 22.3 %all-to-all-done.1 = bf16[128,2,3200]{2,1,0:T(2,128)(2,1)} async-done(((bf16[128,2,3200]{2,1,0:T(2,128)(2,1)}), bf16[128,2,3200]{2,1,0:T(2,128)(2,1)}, u32[]{:S(2)}, u32[]{:S(2)}) %all-to-all-start.1) | async-done | bytes 1638432 | tf_op jit(solution)/shard_map/all_to_all | solution.py:132
  556.5 12.3 %reshape.495 = bf16[2560,10,32]{2,1,0:T(8,128)(2,1)} reshape(bf16[128,2,3200]{2,1,0:T(2,128)(2,1)} %all-to-all-done.1) | data formatting | bytes 3276800
  568.9 37.0 %copy.62 = bf16[20,32,128,10]{3,2,1,0:T(8,128)(2,1)} copy(bf16[20,32,128,10]{1,3,0,2:T(8,128)(2,1)} %bitcast.96) | data formatting | bytes 3276800 | tf_op jit(solution)/shard_map/all_to_all | solution.py:132
  605.9 30.0 %reshape.453 = bf16[320,2560]{1,0:T(8,128)(2,1)} reshape(bf16[20,32,128,10]{3,2,1,0:T(8,128)(2,1)} %copy.62) | data formatting | bytes 3276800 | tf_op jit(solution)/shard_map/reshape | solution.py:133
  638.0 154.4 %while.53 = (s32[]{:T(128)}, bf16[320,5120]{1,0:T(8,128)(2,1)}, s32[1280]{0:T(1024)S(1)}, bf16[320,2560]{1,0:T(8,128)(2,1)}, s32[]{:T(128)}, /*index=5*/s32[]{:T(128)}, s32[]{:T(128)}, s32[]{:T(128)}) while((s32[]{:T(128)}, bf16[320,5120]{1,0:T(8,128)(2,1)}, s32[1280]{0:T(1024)S(1)}, bf16[320,2560]{1,0:T(8,128)(2,1)}, s32[]{:T(128)}, ...), condition=%wide.region_7.8_spmd, body=%wide.region_6.7_spmd.sunk | while | flops 848860672 | bytes 12486795 | solution.py:143
  638.0 12.0 %multiply_convert_fusion.6 = (bf16[1,1280,512]{2,1,0:T(8,128)(2,1)S(1)}, bf16[1,1280,512]{2,1,0:T(8,128)(2,1)S(1)}) fusion(s32[512]{0:T(512)S(1)} %iota_add_fusion.4, s32[1280]{0:T(1024)S(1)} %get-tuple-element.556, f32[1280]{0:T(1024)S(1)} %get-tuple-element.452, f32[1280]{0:T(1024)S(1)} %get-tuple-element.453), kind=kLoop, calls=%fused_computation.15.clone.1 | loop fusion | flops 8519680 | bytes 2638848 | tf_op jit(solution)/shard_map/convert.2
  653.4 12.0 %multiply_convert_fusion.6 = (bf16[1,1280,512]{2,1,0:T(8,128)(2,1)S(1)}, bf16[1,1280,512]{2,1,0:T(8,128)(2,1)S(1)}) fusion(s32[512]{0:T(512)S(1)} %iota_add_fusion.4, s32[1280]{0:T(1024)S(1)} %get-tuple-element.556, f32[1280]{0:T(1024)S(1)} %get-tuple-element.452, f32[1280]{0:T(1024)S(1)} %get-tuple-element.453), kind=kLoop, calls=%fused_computation.15.clone.1 | loop fusion | flops 8519680 | bytes 2638848 | tf_op jit(solution)/shard_map/convert.2
  668.9 12.0 %multiply_convert_fusion.6 = (bf16[1,1280,512]{2,1,0:T(8,128)(2,1)S(1)}, bf16[1,1280,512]{2,1,0:T(8,128)(2,1)S(1)}) fusion(s32[512]{0:T(512)S(1)} %iota_add_fusion.4, s32[1280]{0:T(1024)S(1)} %get-tuple-element.556, f32[1280]{0:T(1024)S(1)} %get-tuple-element.452, f32[1280]{0:T(1024)S(1)} %get-tuple-element.453), kind=kLoop, calls=%fused_computation.15.clone.1 | loop fusion | flops 8519680 | bytes 2638848 | tf_op jit(solution)/shard_map/convert.2
  684.3 12.0 %multiply_convert_fusion.6 = (bf16[1,1280,512]{2,1,0:T(8,128)(2,1)S(1)}, bf16[1,1280,512]{2,1,0:T(8,128)(2,1)S(1)}) fusion(s32[512]{0:T(512)S(1)} %iota_add_fusion.4, s32[1280]{0:T(1024)S(1)} %get-tuple-element.556, f32[1280]{0:T(1024)S(1)} %get-tuple-element.452, f32[1280]{0:T(1024)S(1)} %get-tuple-element.453), kind=kLoop, calls=%fused_computation.15.clone.1 | loop fusion | flops 8519680 | bytes 2638848 | tf_op jit(solution)/shard_map/convert.2
  699.8 12.0 %multiply_convert_fusion.6 = (bf16[1,1280,512]{2,1,0:T(8,128)(2,1)S(1)}, bf16[1,1280,512]{2,1,0:T(8,128)(2,1)S(1)}) fusion(s32[512]{0:T(512)S(1)} %iota_add_fusion.4, s32[1280]{0:T(1024)S(1)} %get-tuple-element.556, f32[1280]{0:T(1024)S(1)} %get-tuple-element.452, f32[1280]{0:T(1024)S(1)} %get-tuple-element.453), kind=kLoop, calls=%fused_computation.15.clone.1 | loop fusion | flops 8519680 | bytes 2638848 | tf_op jit(solution)/shard_map/convert.2
  715.2 12.0 %multiply_convert_fusion.6 = (bf16[1,1280,512]{2,1,0:T(8,128)(2,1)S(1)}, bf16[1,1280,512]{2,1,0:T(8,128)(2,1)S(1)}) fusion(s32[512]{0:T(512)S(1)} %iota_add_fusion.4, s32[1280]{0:T(1024)S(1)} %get-tuple-element.556, f32[1280]{0:T(1024)S(1)} %get-tuple-element.452, f32[1280]{0:T(1024)S(1)} %get-tuple-element.453), kind=kLoop, calls=%fused_computation.15.clone.1 | loop fusion | flops 8519680 | bytes 2638848 | tf_op jit(solution)/shard_map/convert.2
  730.7 12.0 %multiply_convert_fusion.6 = (bf16[1,1280,512]{2,1,0:T(8,128)(2,1)S(1)}, bf16[1,1280,512]{2,1,0:T(8,128)(2,1)S(1)}) fusion(s32[512]{0:T(512)S(1)} %iota_add_fusion.4, s32[1280]{0:T(1024)S(1)} %get-tuple-element.556, f32[1280]{0:T(1024)S(1)} %get-tuple-element.452, f32[1280]{0:T(1024)S(1)} %get-tuple-element.453), kind=kLoop, calls=%fused_computation.15.clone.1 | loop fusion | flops 8519680 | bytes 2638848 | tf_op jit(solution)/shard_map/convert.2
  746.1 12.0 %multiply_convert_fusion.6 = (bf16[1,1280,512]{2,1,0:T(8,128)(2,1)S(1)}, bf16[1,1280,512]{2,1,0:T(8,128)(2,1)S(1)}) fusion(s32[512]{0:T(512)S(1)} %iota_add_fusion.4, s32[1280]{0:T(1024)S(1)} %get-tuple-element.556, f32[1280]{0:T(1024)S(1)} %get-tuple-element.452, f32[1280]{0:T(1024)S(1)} %get-tuple-element.453), kind=kLoop, calls=%fused_computation.15.clone.1 | loop fusion | flops 8519680 | bytes 2638848 | tf_op jit(solution)/shard_map/convert.2
  761.5 12.0 %multiply_convert_fusion.6 = (bf16[1,1280,512]{2,1,0:T(8,128)(2,1)S(1)}, bf16[1,1280,512]{2,1,0:T(8,128)(2,1)S(1)}) fusion(s32[512]{0:T(512)S(1)} %iota_add_fusion.4, s32[1280]{0:T(1024)S(1)} %get-tuple-element.556, f32[1280]{0:T(1024)S(1)} %get-tuple-element.452, f32[1280]{0:T(1024)S(1)} %get-tuple-element.453), kind=kLoop, calls=%fused_computation.15.clone.1 | loop fusion | flops 8519680 | bytes 2638848 | tf_op jit(solution)/shard_map/convert.2
  777.0 12.0 %multiply_convert_fusion.6 = (bf16[1,1280,512]{2,1,0:T(8,128)(2,1)S(1)}, bf16[1,1280,512]{2,1,0:T(8,128)(2,1)S(1)}) fusion(s32[512]{0:T(512)S(1)} %iota_add_fusion.4, s32[1280]{0:T(1024)S(1)} %get-tuple-element.556, f32[1280]{0:T(1024)S(1)} %get-tuple-element.452, f32[1280]{0:T(1024)S(1)} %get-tuple-element.453), kind=kLoop, calls=%fused_computation.15.clone.1 | loop fusion | flops 8519680 | bytes 2638848 | tf_op jit(solution)/shard_map/convert.2
  (129 shorter events, 208.0 us)
Async XLA Ops:
  0.6 17.0 %copy-start.3 = (f32[16]{0:T(128)S(1)}, f32[16]{0:T(128)}, u32[]{:S(2)}) copy-start(f32[16]{0:T(128)} %param.17) | copy-start | bytes 196
  0.6 19.5 %copy-start.2 = (s32[1280]{0:T(1024)S(1)}, s32[1280]{0:T(1024)}, u32[]{:S(2)}) copy-start(s32[1280]{0:T(1024)} %param.16) | copy-start | bytes 15364
  3.1 17.2 %collective-permute-start = (bf16[4,16,5120]{2,1,0:T(8,128)(2,1)}, bf16[4,16,5120]{2,1,0:T(8,128)(2,1)}, u32[]{:S(2)}, u32[]{:S(2)}) collective-permute-start(bf16[4,16,5120]{2,1,0:T(8,128)(2,1)} %get-tuple-element.344), channel_id=1, source_target_pairs={{0,1},{1,2},{2,3},{3,4},{4,5},{5,6},{6,7},{7,8},{8,9},{9,10},{10,1... | collective-permute-start | bytes 1966088 | tf_op jit(solution)/shard_map/ppermute | solution.py:26
  8.0 12.3 %collective-permute-start.1 = (bf16[4,16,5120]{2,1,0:T(8,128)(2,1)}, bf16[4,16,5120]{2,1,0:T(8,128)(2,1)}, u32[]{:S(2)}, u32[]{:S(2)}) collective-permute-start(bf16[4,16,5120]{2,1,0:T(8,128)(2,1)} %get-tuple-element.345), channel_id=1, source_target_pairs={{1,0},{2,1},{3,2},{4,3},{5,4},{6,5},{7,6},{8,7},{9,8},{10,9},{11,1... | collective-permute-start | bytes 1966088 | tf_op jit(solution)/shard_map/ppermute | solution.py:29
  267.3 62.3 %all-to-all-start = ((bf16[128,2,3200]{2,1,0:T(2,128)(2,1)}), bf16[128,2,3200]{2,1,0:T(2,128)(2,1)S(1)}, u32[]{:S(2)}, u32[]{:S(2)}) async-start(bf16[128,2,3200]{2,1,0:T(2,128)(2,1)} %reshape.492), calls=%async_computation | async-start | bytes 3276800 | tf_op jit(solution)/shard_map/all_to_all | solution.py:97
  434.3 2.9 copy-start
  520.7 10.7 %copy-start.1 = (f32[10,32,1280]{2,1,0:T(8,128)S(1)}, f32[10,32,1280]{2,1,0:T(8,128)}, u32[]{:S(2)}) copy-start(f32[10,32,1280]{2,1,0:T(8,128)} %get-tuple-element.269) | copy-start | bytes 4915204
  520.7 35.8 %all-to-all-start.1 = ((bf16[128,2,3200]{2,1,0:T(2,128)(2,1)}), bf16[128,2,3200]{2,1,0:T(2,128)(2,1)}, u32[]{:S(2)}, u32[]{:S(2)}) async-start(bf16[128,2,3200]{2,1,0:T(2,128)(2,1)} %reshape.494), calls=%async_computation.1 | async-start | bytes 3276800 | tf_op jit(solution)/shard_map/all_to_all | solution.py:132
where the time goes:
time: 799 us; the launch traced here: 793 us
  other arithmetic  337 us (42%)
  local copies, waits for them, and re-layouts  232 us (29%)
  matrix products  170 us (21%)
  starting transfers between devices  29.4 us (4%)
  waiting for transfers between devices  22.3 us (3%)
    another operation x20, other arithmetic  237 us
    dot_general x10, matrix products, add_block(): jnp.einsum('mcn,nj->jcm', segment, rows_here, precision=highest)  56.6 us
    mul x1, other arithmetic, basis_rows(): return norm_scale[:, None] * jnp.cos(angles)  50.5 us
    unnamed x13, local copies, waits for them, and re-layouts  47.1 us
    dot_general x10, matrix products, fwd_block(): values = jnp.einsum('jcm,nj->mcn', waves_f, rows_here, precision=highest)  46.9 us
    convert_element_type x2, local copies, waits for them, and re-layouts, per_device(): waves_f = waves_here.astype(jnp.float32)  38.7 us
    gather x4, local copies, waits for them, and re-layouts, per_device(): gathered = grid_view[src_cycle[:, :, k], :, src_block[:, :, k], :]  38.2 us
    all_to_all x1, local copies, waits for them, and re-layouts, per_device(): lax.all_to_all(zonal, ('band', 'set'), split_axis=0, concat_axis=2, tiled...  37 us
  transfers between devices with their start and end apart: 4, of which 1 were waited for; matrix products, arithmetic and copies ran while one was open for 8% of the time, Pallas kernels for 0%

commit v1 on v0

v1 whole, which is shorter than its diff:
```python
import functools
import math

import jax
import jax.numpy as jnp
import ml_dtypes
import numpy as np
from jax import lax
from jax.experimental import pallas as pl
from jax.experimental.pallas import tpu as pltpu
from jax.sharding import PartitionSpec as P

NLAT = 2560
NLON = 5120
MM = 1280
LEV = 8
BW = 128
K = 4
HALO = 4
FL = 16
NB = 40
ROWS = 20
NDEV = 128
OWN = 10
TQ = 5
NG = 10
COLS = 384
MESH = pl.DeviceIdType.MESH
BF = jnp.bfloat16
F32 = jnp.float32


def group_waves(g):
    m2 = np.arange(64)
    if g == 0:
        return 20 * m2, 10 + 20 * m2
    return g + 20 * m2, 20 - g + 20 * m2


@functools.lru_cache(None)
def forward_tables():
    s = math.sqrt(2.0 / NLON)
    i = np.arange(256)
    out = np.zeros((NG, 512, 256))
    for g in range(NG):
        lo, hi = group_waves(g)
        for half, m in ((0, lo), (1, hi)):
            a = 2 * np.pi * ((i[:, None] * m[None, :]) % NLON) / NLON
            c, sn = s * np.cos(a), s * np.sin(a)
            re = slice(64 * half, 64 * half + 64)
            im = slice(128 + 64 * half, 192 + 64 * half)
            if g == 0:
                rows = slice(256 * half, 256 * half + 256)
                out[g, rows, re] = c
                out[g, rows, im] = -sn
            else:
                sign = 1.0 if half == 0 else -1.0
                out[g, :256, re] = c
                out[g, :256, im] = -sn
                out[g, 256:, re] = sign * sn
                out[g, 256:, im] = sign * c
    return out.astype(ml_dtypes.bfloat16)


@functools.lru_cache(None)
def inverse_tables():
    s = math.sqrt(2.0 / NLON)
    i = np.arange(256)
    out = np.zeros((NG, 256, 512))
    for g in range(NG):
        lo, hi = group_waves(g)
        for half, m in ((0, lo), (1, hi)):
            a = 2 * np.pi * ((m[:, None] * i[None, :]) % NLON) / NLON
            w = np.where(m == 0, 0.5, 1.0)[:, None] * s
            c, sn = w * np.cos(a), w * np.sin(a)
            re = slice(64 * half, 64 * half + 64)
            im = slice(128 + 64 * half, 192 + 64 * half)
            if g == 0:
                cols = slice(256 * half, 256 * half + 256)
                out[g, re, cols] = c
                out[g, im, cols] = -sn
            else:
                sign = 1.0 if half == 0 else -1.0
                out[g, re, :256] = c
                out[g, im, :256] = -sn
                out[g, re, 256:] = sign * sn
                out[g, im, 256:] = sign * c
    return out.astype(ml_dtypes.bfloat16)


@functools.lru_cache(None)
def latitude_tables():
    t, r, sl = np.meshgrid(np.arange(TQ), np.arange(4), np.arange(64), indexing="ij")
    j = (20 * sl + 4 * t + r).reshape(-1)
    n = np.arange(MM)
    g = np.where(n == 0, math.sqrt(1.0 / NLAT), math.sqrt(2.0 / NLAT))
    b = g[:, None] * np.cos(np.pi * ((n[:, None] * (2 * j[None, :] + 1)) % (4 * NLAT)) / (2 * NLAT))
    be, bo = b[0::2], b[1::2]
    fwd = np.stack([be, bo]).astype(ml_dtypes.bfloat16)
    bwd = np.stack([be.T, bo.T]).astype(ml_dtypes.bfloat16)
    return np.ascontiguousarray(fwd), np.ascontiguousarray(bwd)


C1, C2 = math.cos(2 * math.pi / 5), math.cos(4 * math.pi / 5)
S1, S2 = math.sin(2 * math.pi / 5), math.sin(4 * math.pi / 5)


def five_parts(x):
    e1, e2 = x[1] + x[4], x[2] + x[3]
    o1, o2 = x[1] - x[4], x[2] - x[3]
    total = x[0] + (e1 + e2)
    return total, x[0] + C1 * e1 + C2 * e2, x[0] + C2 * e1 + C1 * e2, S1 * o1 + S2 * o2, S2 * o1 - S1 * o2


def dft20(d):
    alpha, beta, gr, gi = [], [], [], []
    for q in range(5):
        v = [None] * 4
        for b in (q, q + 5, q + 10, q + 15):
            v[b % 4] = d[b]
        e, o = v[0] + v[2], v[1] + v[3]
        alpha.append(e + o)
        beta.append(e - o)
        gr.append(v[0] - v[2])
        gi.append(v[3] - v[1])
    out = [None] * 11
    s, e1, e2, o1, o2 = five_parts(alpha)
    out[0], out[4], out[8] = (s, None), (e1, -o1), (e2, -o2)
    s, e1, e2, o1, o2 = five_parts(beta)
    out[10], out[6], out[2] = (s, None), (e1, o1), (e2, o2)
    s, e1, e2, o1, o2 = five_parts(gr)
    t, f1, f2, p1, p2 = five_parts(gi)
    out[5] = (s, t)
    out[9] = (e1 + p1, f1 - o1)
    out[1] = (e1 - p1, f1 + o1)
    out[7] = (e2 + p2, o2 - f2)
    out[3] = (e2 - p2, -(f2 + o2))
    return out


def idft20(c):
    a, bb, dr, di = [], [], [], []

    def spread(x0, pr, mi):
        ev1 = x0 + C1 * pr[0] + C2 * pr[1]
        ev2 = x0 + C2 * pr[0] + C1 * pr[1]
        od1 = S1 * mi[0] + S2 * mi[1]
        od2 = S2 * mi[0] - S1 * mi[1]
        return [x0 + (pr[0] + pr[1]), ev1 + od1, ev2 + od2, ev2 - od2, ev1 - od1]

    a = spread(c[0][0], (c[4][0], c[8][0]), (-c[4][1], -c[8][1]))
    bb = spread(c[10][0], (c[6][0], c[2][0]), (c[6][1], c[2][1]))
    dr = spread(
        c[5][0],
        (c[1][0] + c[9][0], c[3][0] + c[7][0]),
        (c[1][1] - c[9][1], c[7][1] - c[3][1]),
    )
    di = spread(
        c[5][1],
        (c[1][1] + c[9][1], -(c[3][1] + c[7][1])),
        (c[9][0] - c[1][0], c[7][0] - c[3][0]),
    )
    plus = [a[q] + bb[q] for q in range(5)]
    minus = [a[q] - bb[q] for q in range(5)]
    out = []
    for b in range(20):
        q = b % 5
        base = plus[q] if b % 2 == 0 else minus[q]
        r = b % 4
        out.append(base + dr[q] if r == 0 else base - di[q] if r == 1 else base - dr[q] if r == 2 else base + di[q])
    return out


def my_index():
    return lax.axis_index("band") * 32 + lax.axis_index("set")


def local_row(me, p):
    return jnp.where(me < NDEV // 2, p, ROWS - 1 - p)


def slot_of(d):
    return jnp.where(d < NDEV // 2, d, 3 * NDEV // 2 - 1 - d)


def one_hot(nat_ref, out_ref):
    def chunk(i, c):
        rows = pl.ds(pl.multiple_of(i * 128, 128), 128)
        lanes = lax.broadcasted_iota(jnp.int32, (128, MM), 1)
        out_ref[rows, :] = jnp.where(nat_ref[rows, :] == lanes, 1.0, 0.0).astype(BF)
        return c

    lax.fori_loop(0, NB // 4, chunk, 0)


def grid_kernel(lo_ref, mid_ref, hi_ref, dep_ref, blend_ref, nat_ref, tab_ref, out_ref,
                src, dep_f, g_buf, f_buf, hot, sem):
    me = my_index()
    copies = []
    for part, (ref, first, count) in enumerate(((lo_ref, 0, HALO), (mid_ref, HALO, ROWS), (hi_ref, HALO + ROWS, HALO))):
        for b in range(NB):
            copies.append(pltpu.make_async_copy(
                ref.at[:, :, pl.ds(b * BW, BW)], src.at[pl.ds(first, count), b], sem.at[part * NB + b]))
    for c in copies:
        c.start()
    one_hot(nat_ref, hot)
    for c in copies:
        c.wait()
    base = (me * ROWS - HALO) * NB

    def cycle(p, carry):
        r = local_row(me, p)
        for b in range(NB):
            total = None
            for k in range(K):
                at = dep_ref[(r * NB + b) * K + k] - base
                cyc = at // NB
                tile = src[cyc, at - cyc * NB].astype(F32)
                term = blend_ref[r, b, pl.ds(k, 1), :] * tile
                total = term if total is None else total + term
            dep_f[b // 2, :, pl.ds((b % 2) * BW, BW)] = total
        rows = pl.ds(pl.multiple_of(p * FL, FL), FL)
        for half in range(2):
            lanes = pl.ds(half * 128, 128)
            g = dft20([dep_f[b, :, lanes] for b in range(20)])
            pairs = [(g[0][0], g[10][0])] + [g[i] for i in range(1, 10)]
            for i, (re, im) in enumerate(pairs):
                g_buf[i, rows, pl.ds(half * 128, 128)] = re.astype(BF)
                g_buf[i, rows, pl.ds(256 + half * 128, 128)] = im.astype(BF)
        return carry

    lax.fori_loop(0, ROWS, cycle, 0)

    def group(g, carry):
        v = jnp.dot(g_buf[g], tab_ref[g], preferred_element_type=F32).astype(BF)
        lanes = pl.ds(pl.multiple_of(g * 128, 128), 128)
        f_buf[:, 0, :, lanes] = v[:, :128].reshape(ROWS, FL, 128)
        f_buf[:, 1, :, lanes] = v[:, 128:].reshape(ROWS, FL, 128)
        return carry

    lax.fori_loop(0, NG, group, 0)

    def order(i, carry):
        rows = pl.ds(pl.multiple_of(i * 256, 256), 256)
        v = lax.dot_general(hot[rows, :], f_buf[...].reshape(ROWS * 32, MM), (((1,), (1,)), ((), ())),
                            preferred_element_type=F32).astype(BF)
        for t in range(TQ):
            out_ref[t, rows, :] = v[:, t * 128:(t + 1) * 128]
        return carry

    lax.fori_loop(0, MM // 256, order, 0)


def block_swap(x):
    lane = lax.broadcasted_iota(jnp.int32, x[0].shape, 1)
    low64 = lane < 64
    low32 = (lane % 64) < 32
    z = [None] * 4
    for a in range(2):
        lo, hi = x[a], x[a + 2]
        z[a] = jnp.where(low64, lo, pltpu.roll(hi, 64, 1))
        z[a + 2] = jnp.where(low64, pltpu.roll(lo, 64, 1), hi)
    y = [None] * 4
    for a in (0, 2):
        lo, hi = z[a], z[a + 1]
        y[a] = jnp.where(low32, lo, pltpu.roll(hi, 32, 1))
        y[a + 1] = jnp.where(low32, pltpu.roll(lo, 96, 1), hi)
    return y


def lat_kernel(x_ref, fwd_ref, bwd_ref, damp_ref, wave_ref, spec_ref, out_ref, xf, uv, sbuf, s16, zf):
    def widen(i, c):
        rows = pl.ds(pl.multiple_of(i * 256, 256), 256)
        xf[rows, :] = x_ref[rows, :].astype(F32)
        return c

    lax.fori_loop(0, 25, widen, 0)

    def fold(i, carry):
        t, sc = i // 4, i % 4
        for g in range(3):
            us, vs = [], []
            for m in range(4 * g, 4 * g + 4):
                if m >= OWN:
                    us.append(jnp.zeros((16, 128), F32))
                    vs.append(jnp.zeros((16, 128), F32))
                    continue
                lo = xf[pl.ds(sc * 16 * 50 + t * OWN + m, 16, stride=50), :]
                hi = xf[pl.ds((64 + sc * 16) * 50 + t * OWN + m, 16, stride=50), :]
                us.append(lo + hi)
                vs.append(lo - hi)
            for par, vals in ((0, us), (1, vs)):
                y = block_swap(vals)
                for r in range(4):
                    rows = pl.ds(pl.multiple_of((t * 4 + r) * 64 + sc * 16, 16), 16)
                    uv[par, rows, pl.ds(g * 128, 128)] = y[r].astype(BF)
        return carry

    lax.fori_loop(0, 20, fold, 0)

    lane = lax.broadcasted_iota(jnp.int32, (1, COLS), 1)
    squared = (lane % FL) < LEV

    def analyse(i, carry):
        rows = pl.ds(pl.multiple_of(i * 128, 128), 128)
        for par in range(2):
            v = jnp.dot(fwd_ref[par, rows, :], uv[par], preferred_element_type=F32)
            n = 2 * (i * 128 + lax.broadcasted_iota(jnp.int32, (128, COLS), 0)) + par
            nf = n.astype(F32)
            q = nf * (nf + 1.0) * (1.0 / (MM * (MM - 1.0)))
            qp = jnp.where(squared, q * q, q)
            v = v * (1.0 / (1.0 + damp_ref[...] * qp))
            v = jnp.where(n >= wave_ref[...], v, 0.0)
            sbuf[pl.ds(i * 256 + par, 128, stride=2), :] = v[:, :128]
            sbuf[pl.ds(MM + i * 256 + par, 128, stride=2), :] = v[:, 128:256]
            sbuf[pl.ds(2 * MM + i * 256 + par, 128, stride=2), :] = v[:, 256:]
            s16[par, rows, :] = v.astype(BF)
        return carry

    lax.fori_loop(0, 5, analyse, 0)

    def synth(t, carry):
        rows = pl.ds(pl.multiple_of(t * 256, 256), 256)
        p = jnp.dot(bwd_ref[0, rows, :], s16[0], preferred_element_type=F32)
        q = jnp.dot(bwd_ref[1, rows, :], s16[1], preferred_element_type=F32)
        for half, z in ((0, p + q), (1, p - q)):
            for g in range(3):
                y = block_swap([z[r * 64:(r + 1) * 64, g * 128:(g + 1) * 128] for r in range(4)])
                for m in range(4 * g, min(4 * g + 4, OWN)):
                    zf[pl.ds(half * 64 * 50 + t * OWN + m, 64, stride=50), :] = y[m - 4 * g]
        return carry

    lax.fori_loop(0, TQ, synth, 0)

    def narrow(i, c):
        rows = pl.ds(pl.multiple_of(i * 256, 256), 256)
        out_ref[rows, :] = zf[rows, :].astype(BF)
        return c

    lax.fori_loop(0, 25, narrow, 0)

    for g in range(3):
        for nt in range(10):
            tr = jnp.transpose(sbuf[pl.ds(g * MM + nt * 128, 128), :])
            for m in range(4 * g, min(4 * g + 4, OWN)):
                for c in range(2):
                    first = (m - 4 * g) * 32 + c * 16
                    spec_ref[m, :, c, pl.ds(nt * 128, 128)] = tr[first:first + 16]


def wave_kernel(x_ref, nat_ref, tab_ref, out_ref, zt, hot, zn, h_buf):
    me = my_index()
    one_hot(nat_ref, hot)

    def turn(t, carry):
        zt[pl.ds(pl.multiple_of(t * 128, 128), 128), :] = jnp.transpose(x_ref[t])
        return carry

    lax.fori_loop(0, TQ, turn, 0)

    def order(i, carry):
        lanes = pl.ds(pl.multiple_of(i * 256, 256), 256)
        v = jnp.dot(zt[...], hot[:, lanes], preferred_element_type=F32).astype(BF)
        zn[:, :, :, lanes] = v.reshape(ROWS, 2, FL, 256)
        return carry

    lax.fori_loop(0, MM // 256, order, 0)

    def group(g, carry):
        lanes = pl.ds(pl.multiple_of(g * 128, 128), 128)
        re = zn[:, 0, :, lanes].reshape(ROWS * FL, 128)
        im = zn[:, 1, :, lanes].reshape(ROWS * FL, 128)
        v = jnp.concatenate([re, im], axis=1)
        h_buf[g] = jnp.dot(v, tab_ref[g], preferred_element_type=F32)
        return carry

    lax.fori_loop(0, NG, group, 0)

    def cycle(p, carry):
        r = local_row(me, p)
        rows = pl.ds(pl.multiple_of(p * FL, FL), FL)
        for half in range(2):
            re = [h_buf[g, rows, pl.ds(half * 128, 128)] for g in range(NG)]
            im = [h_buf[g, rows, pl.ds(256 + half * 128, 128)] for g in range(NG)]
            c = [(re[0], None)] + [(re[g], im[g]) for g in range(1, NG)] + [(im[0], None)]
            y = idft20(c)
            for b in range(20):
                out_ref[r, :, pl.ds(b * 256 + half * 128, 128)] = y[b].astype(BF)
        return carry

    lax.fori_loop(0, ROWS, cycle, 0)


def partner(i):
    x = lax.axis_index("band")
    st = lax.axis_index("set")
    j = lax.rem(i * 37, NDEV)
    tx = lax.rem(x + j // 32, 4)
    ty = lax.rem(st // 8 + lax.rem(j // 8, 4), 4)
    tz = lax.rem(lax.rem(st // 2, 4) + lax.rem(j // 2, 4), 4)
    tc = lax.rem(lax.rem(st, 2) + lax.rem(j, 2), 2)
    return tx, (ty * 4 + tz) * 2 + tc


def exchange_kernel(to_owner, x_ref, o_ref, ssem, rsem, lsem):
    me = my_index()

    def ends(d):
        if to_owner:
            return x_ref.at[:, pl.ds(d * 5, 5)], o_ref.at[slot_of(me)]
        return x_ref.at[slot_of(d)], o_ref.at[:, pl.ds(me * 5, 5)]

    own = pltpu.make_async_copy(*ends(me), lsem)
    own.start()

    def copy(i):
        tx, ts = partner(i)
        src, dst = ends(tx * 32 + ts)
        return pltpu.make_async_remote_copy(
            src_ref=src, dst_ref=dst, send_sem=ssem.at[i], recv_sem=rsem.at[i],
            device_id=(tx, ts), device_id_type=MESH)

    def start(i, c):
        copy(i).start()
        return c

    def wait(i, c):
        copy(i).wait()
        return c

    lax.fori_loop(1, NDEV, start, 0)
    own.wait()
    lax.fori_loop(1, NDEV, wait, 0)


ANY = pl.BlockSpec(memory_space=pl.ANY)
VM = pl.BlockSpec(memory_space=pltpu.VMEM)
SM = pl.BlockSpec(memory_space=pltpu.SMEM)
LIMIT = 56 * 2**20


def exchange(x, shape, to_owner, name):
    return pl.pallas_call(
        functools.partial(exchange_kernel, to_owner),
        out_shape=jax.ShapeDtypeStruct(shape, BF),
        in_specs=[ANY],
        out_specs=ANY,
        scratch_shapes=[pltpu.SemaphoreType.DMA((NDEV,)), pltpu.SemaphoreType.DMA((NDEV,)), pltpu.SemaphoreType.DMA],
        compiler_params=pltpu.CompilerParams(has_side_effects=True),
        name=name,
    )(x)


def per_device(fields, depart, blend, wave_owner, damping):
    me = my_index()
    count = NDEV
    low = lax.ppermute(fields[ROWS - HALO:], ("band", "set"), [(i, i + 1) for i in range(count - 1)])
    high = lax.ppermute(fields[:HALO], ("band", "set"), [(i + 1, i) for i in range(count - 1)])
    m1, m2 = wave_owner % 20, wave_owner // 20
    grp = jnp.where(m1 == 10, 0, jnp.minimum(m1, 20 - m1) % 20)
    nat = (grp * 128 + jnp.where(m1 >= 10, 64, 0) + m2).astype(jnp.int32)[:, None]
    owned = lax.dynamic_slice_in_dim(wave_owner, me * OWN, OWN, 0)
    wave_lane = jnp.pad(jnp.repeat(owned, 32), (0, COLS - 32 * OWN), constant_values=MM)[None, :]
    damp_lane = jnp.tile(damping, COLS // FL)[None, :]
    fwd_lat, bwd_lat = latitude_tables()
    sent = pl.pallas_call(
        grid_kernel,
        out_shape=jax.ShapeDtypeStruct((TQ, MM, 128), BF),
        in_specs=[ANY, ANY, ANY, SM, VM, VM, VM],
        out_specs=VM,
        scratch_shapes=[
            pltpu.VMEM((ROWS + 2 * HALO, NB, FL, BW), BF),
            pltpu.VMEM((20, FL, 256), F32),
            pltpu.VMEM((NG, ROWS * FL, 512), BF),
            pltpu.VMEM((ROWS, 2, FL, MM), BF),
            pltpu.VMEM((MM, MM), BF),
            pltpu.SemaphoreType.DMA((3 * NB,)),
        ],
        compiler_params=pltpu.CompilerParams(vmem_limit_bytes=LIMIT),
        name="grid_step",
    )(low, fields, high, depart.reshape(-1), blend, nat, jnp.asarray(forward_tables()))
    got = exchange(sent.reshape(TQ, MM // 2, 2, 128), (NDEV, TQ, 5, 2, 128), True, "to_owner")
    spectra, back = pl.pallas_call(
        lat_kernel,
        out_shape=(jax.ShapeDtypeStruct((OWN, FL, 2, MM), F32), jax.ShapeDtypeStruct((NDEV * 50, 128), BF)),
        in_specs=[VM] * 5,
        out_specs=(VM, VM),
        scratch_shapes=[
            pltpu.VMEM((NDEV * 50, 128), F32),
            pltpu.VMEM((2, NLAT // 2, COLS), BF),
            pltpu.VMEM((3 * MM, 128), F32),
            pltpu.VMEM((2, MM // 2, COLS), BF),
            pltpu.VMEM((NDEV * 50, 128), F32),
        ],
        compiler_params=pltpu.CompilerParams(vmem_limit_bytes=LIMIT),
        name="latitude_step",
    )(got.reshape(NDEV * 50, 128), jnp.asarray(fwd_lat), jnp.asarray(bwd_lat), damp_lane, wave_lane)
    zonal = exchange(back.reshape(NDEV, TQ, 5, 2, 128), (TQ, MM // 2, 2, 128), False, "to_cycles")
    updated = pl.pallas_call(
        wave_kernel,
        out_shape=jax.ShapeDtypeStruct((ROWS, FL, NLON), BF),
        in_specs=[VM] * 3,
        out_specs=VM,
        scratch_shapes=[
            pltpu.VMEM((ROWS * 32, MM), BF),
            pltpu.VMEM((MM, MM), BF),
            pltpu.VMEM((ROWS, 2, FL, MM), BF),
            pltpu.VMEM((NG, ROWS * FL, 512), F32),
        ],
        compiler_params=pltpu.CompilerParams(vmem_limit_bytes=LIMIT),
        name="wave_step",
    )(zonal.reshape(TQ, MM, 128), nat, jnp.asarray(inverse_tables()))
    return (updated, spectra)


def solution(mesh):
    in_specs = (
        P(("band", "set"), None, None),
        P(("band", "set"), None, None),
        P(("band", "set"), None, None, None),
        P(),
        P(),
    )
    out_specs = (P(("band", "set"), None, None), P(("band", "set"), None, None, None))
    return jax.shard_map(
        per_device, mesh=mesh, in_specs=in_specs, out_specs=out_specs, check_vma=False
    )
```

time: 799 us -> 161 us (0.20)
  other arithmetic: 337 us -> 0.03 us
  local copies, waits for them, and re-layouts: 232 us -> 5.89 us
  matrix products: 170 us -> 0 us
  Pallas kernels: 0 us -> 143 us
  starting transfers between devices: 29.4 us -> 6.86 us
  waiting for transfers between devices: 22.3 us -> 3.8 us
    another operation x40 -> x0, other arithmetic: 257 us -> none
    dot_general x40 -> x0, matrix products: 170 us -> none  [the longest x10 56.6 us: add_block(): jnp.einsum('mcn,nj->jcm', segment, rows_here, precision=highest)]
    pallas_call x0 -> x5, Pallas kernels: none -> 143 us  [the longest x2 74.3 us: exchange(): pl.pallas_call(functools.partial(exchange_kernel, to_owner), out_shape=ja...]
    mul x13 -> x0, other arithmetic: 55.3 us -> none  [the longest x1 50.5 us: basis_rows(): return norm_scale[:, None] * jnp.cos(angles)]
    convert_element_type x4 -> x0, local copies, waits for them, and re-layouts: 51.3 us -> none  [the longest x2 38.7 us: per_device(): waves_f = waves_here.astype(jnp.float32)]
    unnamed x13 -> x11, local copies, waits for them, and re-layouts: 47.1 us -> 1.07 us
    reshape x4 -> x2, local copies, waits for them, and re-layouts: 43.8 us -> 0.91 us  [the longest x1 0.83 us: per_device(): depart.reshape(-1)]
    gather x4 -> x0, local copies, waits for them, and re-layouts: 38.2 us -> none  [per_device(): gathered = grid_view[src_cycle[:, :, k], :, src_block[:, :, k], :]]
  transfers between devices with their start and end apart: 4 -> 2, of which waited for: 1 -> 2; matrix products, arithmetic and copies ran while one was open for 8% -> 2% of each run, Pallas kernels for 0% -> 0%
where the time goes in v1:
time: 161 us
  Pallas kernels  143 us (89%)
  starting transfers between devices  6.86 us (4%)
  local copies, waits for them, and re-layouts  5.89 us (4%)
  waiting for transfers between devices  3.8 us (2%)
    pallas_call x2, Pallas kernels, exchange(): pl.pallas_call(functools.partial(exchange_kernel, to_owner), out_shape=ja...  74.3 us
    pallas_call x1, Pallas kernels, per_device(): pl.pallas_call(grid_kernel, out_shape=jax.ShapeDtypeStruct((TQ, MM, 128),...  38.9 us
    pallas_call x1, Pallas kernels, per_device(): pl.pallas_call(lat_kernel, out_shape=(jax.ShapeDtypeStruct((OWN, FL, 2, M...  16.9 us
    pallas_call x1, Pallas kernels, per_device(): pl.pallas_call(wave_kernel, out_shape=jax.ShapeDtypeStruct((ROWS, FL, NLO...  13.3 us
    ppermute x1, starting transfers between devices, per_device(): lax.ppermute(fields[ROWS - HALO:], ('band', 'set'), [(i, i + 1) for i in...  3.53 us
    ppermute x1, starting transfers between devices, per_device(): lax.ppermute(fields[:HALO], ('band', 'set'), [(i + 1, i) for i in range(c...  3.33 us
  transfers between devices with their start and end apart: 2, of which 2 were waited for; matrix products, arithmetic and copies ran while one was open for 2% of the time, Pallas kernels for 0%

profile of v1, /device:TPU:1, one launch (start us, length us, event | category | flops | bytes accessed | tf_op | source)
XLA Modules:
  0.0 160.7 jit_solution(8512759952668446274)
XLA Ops:
  0.6 0.0 copy-start.3
  0.6 0.0 copy-start.4
  0.7 0.0 copy-start.2
  0.7 1.4 fusion.7
  2.1 3.3 %collective-permute-start.1 = (bf16[4,16,5120]{2,1,0:T(8,128)(2,1)S(1)}, bf16[4,16,5120]{2,1,0:T(8,128)(2,1)S(1)}, u32[]{:S(2)}, u32[]{:S(2)}) collective-permute-start(bf16[4,16,5120]{2,1,0:T(8,128)(2,1)S(1)} %get-tuple-element.6), channel_id=1, source_target_pairs={{1,0},{2,1},{3,2},{4,3},{5,4},{6,5},{7,6},{8,7},{9,8},{10,9},{11,1... | collective-permute-start | bytes 1966088 | tf_op jit(solution)/shard_map/ppermute | solution.py:458
  5.4 3.5 %collective-permute-start = (bf16[4,16,5120]{2,1,0:T(8,128)(2,1)S(1)}, bf16[4,16,5120]{2,1,0:T(8,128)(2,1)S(1)}, u32[]{:S(2)}, u32[]{:S(2)}) collective-permute-start(bf16[4,16,5120]{2,1,0:T(8,128)(2,1)S(1)} %get-tuple-element.7), channel_id=1, source_target_pairs={{0,1},{1,2},{2,3},{3,4},{4,5},{5,6},{6,7},{7,8},{8,9},{9,10},{10,1... | collective-permute-start | bytes 1966088 | tf_op jit(solution)/shard_map/ppermute | solution.py:457
  8.9 0.0 copy-done.3
  8.9 0.1 dynamic_slice.3
  9.0 0.1 broadcast_in_dim.19
  9.1 0.1 reshape.26
  9.2 0.6 broadcast_in_dim.20.wave_ref
  9.8 0.0 copy-done.4
  9.8 0.7 broadcast_in_dim_tile.3.damp_ref
  10.4 0.0 copy-done.2
  10.5 0.2 copy.11
  10.7 0.8 reshape.23.dep_ref
  11.5 1.1 broadcast_in_dim.21.nat_ref
  12.6 2.6 %collective-permute-done.1.hi_ref = bf16[4,16,5120]{2,1,0:T(8,128)(2,1)S(1)} collective-permute-done((bf16[4,16,5120]{2,1,0:T(8,128)(2,1)S(1)}, bf16[4,16,5120]{2,1,0:T(8,128)(2,1)S(1)}, u32[]{:S(2)}, u32[]{:S(2)}) %collective-permute-start.1) | collective-permute-done | bytes 655392 | tf_op jit(solution)/shard_map/ppermute | solution.py:458
  15.3 0.0 copy-start
  15.3 1.2 collective-permute-done.lo_ref
  16.4 0.0 copy-done
  16.4 0.0 copy-start.1
  16.4 0.8 copy-done.1
  17.3 38.9 %grid_step.1 = bf16[5,1280,128]{2,1,0:T(8,128)(2,1)} custom-call(bf16[4,16,5120]{2,1,0:T(8,128)(2,1)} %copy-done.1, bf16[20,16,5120]{2,1,0:T(8,128)(2,1)} %mid_ref.1, bf16[4,16,5120]{2,1,0:T(8,128)(2,1)} %copy-done, s32[3200]{0:T(1024)} %reshape.23.dep_ref, f32[20,40,4,128]{3,2,1,0:T(4,128)} %blend_ref.1, s32[1280,1]{1,0:T(8,128)} %broadcast_in_dim.21.nat_ref, ...), custom_call_target="tpu_custom_call" | custom-call | tf_op jit(solution)/shard_map/grid_step/pallas_call | solution.py:466
  56.2 42.3 %to_owner.1 = bf16[128,5,5,2,128]{4,3,2,1,0:T(2,128)(2,1)} custom-call(bf16[5,640,2,128]{3,2,1,0:T(2,128)(2,1)} %bitcast.5), custom_call_target="tpu_custom_call" | custom-call | tf_op jit(solution)/shard_map/to_owner/pallas_call | solution.py:443
  98.5 16.9 %latitude_step.1 = (f32[10,16,2,1280]{3,2,1,0:T(2,128)}, bf16[6400,128]{1,0:T(8,128)(2,1)}) custom-call(bf16[6400,128]{1,0:T(8,128)(2,1)} %bitcast.4, bf16[2,640,1280]{2,1,0:T(8,128)(2,1)} %constant.54.clone.fwd_ref, bf16[2,1280,640]{2,1,0:T(8,128)(2,1)} %constant.55.clone.bwd_ref, f32[1,384]{1,0:T(1,128)} %broadcast_in_dim_tile.3.damp_ref, ...), custom_call_target="tpu_custom_call" | custom-call | tf_op jit(solution)/shard_map/latitude_step/pallas_call | solution.py:483
  115.4 32.0 %to_cycles.1 = bf16[5,640,2,128]{3,2,1,0:T(2,128)(2,1)} custom-call(bf16[128,5,5,2,128]{4,3,2,1,0:T(2,128)(2,1)} %bitcast.7), custom_call_target="tpu_custom_call" | custom-call | tf_op jit(solution)/shard_map/to_cycles/pallas_call | solution.py:443
  147.4 13.3 %wave_step.1 = bf16[20,16,5120]{2,1,0:T(8,128)(2,1)} custom-call(bf16[5,1280,128]{2,1,0:T(8,128)(2,1)} %bitcast.6, s32[1280,1]{1,0:T(8,128)} %broadcast_in_dim.21.nat_ref, bf16[10,256,512]{2,1,0:T(8,128)(2,1)} %constant.56.clone.tab_ref), custom_call_target="tpu_custom_call" | custom-call | tf_op jit(solution)/shard_map/wave_step/pallas_call | solution.py:499
  (3 shorter events, 0.0 us)
Async XLA Ops:
  0.6 8.3 %copy-start.3 = (s32[1280]{0:T(1024)S(1)}, s32[1280]{0:T(1024)}, u32[]{:S(2)}) copy-start(s32[1280]{0:T(1024)} %param.12) | copy-start | bytes 15364
  0.6 9.1 %copy-start.4 = (f32[16]{0:T(128)S(1)}, f32[16]{0:T(128)}, u32[]{:S(2)}) copy-start(f32[16]{0:T(128)} %param.13) | copy-start | bytes 196
  0.7 9.8 %copy-start.2 = (s32[20,40,4]{1,2,0:T(4,128)S(1)}, s32[20,40,4]{1,2,0:T(4,128)}, u32[]{:S(2)}) copy-start(s32[20,40,4]{1,2,0:T(4,128)} %param.10) | copy-start | bytes 38404
  2.1 13.2 %collective-permute-start.1 = (bf16[4,16,5120]{2,1,0:T(8,128)(2,1)S(1)}, bf16[4,16,5120]{2,1,0:T(8,128)(2,1)S(1)}, u32[]{:S(2)}, u32[]{:S(2)}) collective-permute-start(bf16[4,16,5120]{2,1,0:T(8,128)(2,1)S(1)} %get-tuple-element.6), channel_id=1, source_target_pairs={{1,0},{2,1},{3,2},{4,3},{5,4},{6,5},{7,6},{8,7},{9,8},{10,9},{11,1... | collective-permute-start | bytes 1966088 | tf_op jit(solution)/shard_map/ppermute | solution.py:458
  5.4 11.0 %collective-permute-start = (bf16[4,16,5120]{2,1,0:T(8,128)(2,1)S(1)}, bf16[4,16,5120]{2,1,0:T(8,128)(2,1)S(1)}, u32[]{:S(2)}, u32[]{:S(2)}) collective-permute-start(bf16[4,16,5120]{2,1,0:T(8,128)(2,1)S(1)} %get-tuple-element.7), channel_id=1, source_target_pairs={{0,1},{1,2},{2,3},{3,4},{4,5},{5,6},{6,7},{7,8},{8,9},{9,10},{10,1... | collective-permute-start | bytes 1966088 | tf_op jit(solution)/shard_map/ppermute | solution.py:457
  15.3 1.2 copy-start
  16.4 0.8 copy-start.1

commit v2 on v1

v2 whole, which is shorter than its diff:
```python
import functools
import math

import jax
import jax.numpy as jnp
import ml_dtypes
import numpy as np
from jax import lax
from jax.experimental import pallas as pl
from jax.experimental.pallas import tpu as pltpu
from jax.sharding import PartitionSpec as P

NLAT = 2560
NLON = 5120
MM = 1280
LEV = 8
BW = 128
K = 4
HALO = 4
FL = 16
NB = 40
ROWS = 20
NDEV = 128
OWN = 10
TQ = 5
NG = 10
COLS = 384
MESH = pl.DeviceIdType.MESH
BF = jnp.bfloat16
F32 = jnp.float32


def group_waves(g):
    m2 = np.arange(64)
    if g == 0:
        return 20 * m2, 10 + 20 * m2
    return g + 20 * m2, 20 - g + 20 * m2


@functools.lru_cache(None)
def forward_tables():
    s = math.sqrt(2.0 / NLON)
    i = np.arange(256)
    out = np.zeros((NG, 512, 256))
    for g in range(NG):
        lo, hi = group_waves(g)
        for half, m in ((0, lo), (1, hi)):
            a = 2 * np.pi * ((i[:, None] * m[None, :]) % NLON) / NLON
            c, sn = s * np.cos(a), s * np.sin(a)
            re = slice(64 * half, 64 * half + 64)
            im = slice(128 + 64 * half, 192 + 64 * half)
            if g == 0:
                rows = slice(256 * half, 256 * half + 256)
                out[g, rows, re] = c
                out[g, rows, im] = -sn
            else:
                sign = 1.0 if half == 0 else -1.0
                out[g, :256, re] = c
                out[g, :256, im] = -sn
                out[g, 256:, re] = sign * sn
                out[g, 256:, im] = sign * c
    return out.astype(ml_dtypes.bfloat16)


@functools.lru_cache(None)
def inverse_tables():
    s = math.sqrt(2.0 / NLON)
    i = np.arange(256)
    out = np.zeros((NG, 256, 512))
    for g in range(NG):
        lo, hi = group_waves(g)
        for half, m in ((0, lo), (1, hi)):
            a = 2 * np.pi * ((m[:, None] * i[None, :]) % NLON) / NLON
            w = np.where(m == 0, 0.5, 1.0)[:, None] * s
            c, sn = w * np.cos(a), w * np.sin(a)
            re = slice(64 * half, 64 * half + 64)
            im = slice(128 + 64 * half, 192 + 64 * half)
            if g == 0:
                cols = slice(256 * half, 256 * half + 256)
                out[g, re, cols] = c
                out[g, im, cols] = -sn
            else:
                sign = 1.0 if half == 0 else -1.0
                out[g, re, :256] = c
                out[g, im, :256] = -sn
                out[g, re, 256:] = sign * sn
                out[g, im, 256:] = sign * c
    return out.astype(ml_dtypes.bfloat16)


@functools.lru_cache(None)
def latitude_tables():
    c, t, r, sl = np.meshgrid(np.arange(4), np.arange(TQ), np.arange(4), np.arange(16), indexing="ij")
    j = (20 * (4 * sl + c) + 4 * t + r).reshape(-1)
    n = np.arange(MM)
    g = np.where(n == 0, math.sqrt(1.0 / NLAT), math.sqrt(2.0 / NLAT))
    b = g[:, None] * np.cos(np.pi * ((n[:, None] * (2 * j[None, :] + 1)) % (4 * NLAT)) / (2 * NLAT))
    be, bo = b[0::2], b[1::2]
    fwd = np.stack([be, bo]).astype(ml_dtypes.bfloat16)
    bwd = np.stack([be.T, bo.T]).astype(ml_dtypes.bfloat16)
    return np.ascontiguousarray(fwd), np.ascontiguousarray(bwd)


C1, C2 = math.cos(2 * math.pi / 5), math.cos(4 * math.pi / 5)
S1, S2 = math.sin(2 * math.pi / 5), math.sin(4 * math.pi / 5)


def five_parts(x):
    e1, e2 = x[1] + x[4], x[2] + x[3]
    o1, o2 = x[1] - x[4], x[2] - x[3]
    total = x[0] + (e1 + e2)
    return total, x[0] + C1 * e1 + C2 * e2, x[0] + C2 * e1 + C1 * e2, S1 * o1 + S2 * o2, S2 * o1 - S1 * o2


def dft20(d):
    alpha, beta, gr, gi = [], [], [], []
    for q in range(5):
        v = [None] * 4
        for b in (q, q + 5, q + 10, q + 15):
            v[b % 4] = d[b]
        e, o = v[0] + v[2], v[1] + v[3]
        alpha.append(e + o)
        beta.append(e - o)
        gr.append(v[0] - v[2])
        gi.append(v[3] - v[1])
    out = [None] * 11
    s, e1, e2, o1, o2 = five_parts(alpha)
    out[0], out[4], out[8] = (s, None), (e1, -o1), (e2, -o2)
    s, e1, e2, o1, o2 = five_parts(beta)
    out[10], out[6], out[2] = (s, None), (e1, o1), (e2, o2)
    s, e1, e2, o1, o2 = five_parts(gr)
    t, f1, f2, p1, p2 = five_parts(gi)
    out[5] = (s, t)
    out[9] = (e1 + p1, f1 - o1)
    out[1] = (e1 - p1, f1 + o1)
    out[7] = (e2 + p2, o2 - f2)
    out[3] = (e2 - p2, -(f2 + o2))
    return out


def idft20(c):
    a, bb, dr, di = [], [], [], []

    def spread(x0, pr, mi):
        ev1 = x0 + C1 * pr[0] + C2 * pr[1]
        ev2 = x0 + C2 * pr[0] + C1 * pr[1]
        od1 = S1 * mi[0] + S2 * mi[1]
        od2 = S2 * mi[0] - S1 * mi[1]
        return [x0 + (pr[0] + pr[1]), ev1 + od1, ev2 + od2, ev2 - od2, ev1 - od1]

    a = spread(c[0][0], (c[4][0], c[8][0]), (-c[4][1], -c[8][1]))
    bb = spread(c[10][0], (c[6][0], c[2][0]), (c[6][1], c[2][1]))
    dr = spread(
        c[5][0],
        (c[1][0] + c[9][0], c[3][0] + c[7][0]),
        (c[1][1] - c[9][1], c[7][1] - c[3][1]),
    )
    di = spread(
        c[5][1],
        (c[1][1] + c[9][1], -(c[3][1] + c[7][1])),
        (c[9][0] - c[1][0], c[7][0] - c[3][0]),
    )
    plus = [a[q] + bb[q] for q in range(5)]
    minus = [a[q] - bb[q] for q in range(5)]
    out = []
    for b in range(20):
        q = b % 5
        base = plus[q] if b % 2 == 0 else minus[q]
        r = b % 4
        out.append(base + dr[q] if r == 0 else base - di[q] if r == 1 else base - dr[q] if r == 2 else base + di[q])
    return out


def my_index():
    return lax.axis_index("band") * 32 + lax.axis_index("set")


def local_row(me, p):
    return jnp.where(me < NDEV // 2, p, ROWS - 1 - p)


def place_of(d):
    far = d // (NDEV // 2)
    s = d + far * (NDEV - 1 - 2 * d)
    return far * 64 + (s % 4) * 16 + s // 4


def nat_columns(wave_ref, out_ref):
    w = wave_ref[...]
    m2 = w // 20
    m1 = w - 20 * m2
    grp = jnp.where(m1 > 10, 20 - m1, jnp.where(m1 == 10, 0, m1))
    nat = (grp * 128 + jnp.where(m1 >= 10, 64, 0) + m2).astype(F32)
    for i in range(MM // 128):
        out_ref[pl.ds(i * 128, 128), :] = jnp.transpose(
            jnp.broadcast_to(nat[:, i * 128:(i + 1) * 128], (128, 128)))


def one_hot(nat, first, count):
    lanes = first + lax.broadcasted_iota(jnp.int32, nat.shape, 1).astype(F32)
    return jnp.concatenate(
        [jnp.where(nat == lanes + 128.0 * j, 1.0, 0.0).astype(BF) for j in range(count // 128)], axis=1)


def device_of(index):
    return index // 32, index % 32


def grid_kernel(fields_ref, dep_ref, blend_hbm, tab_hbm, out_ref,
                mid, top, low, blend_v, tab_v, dep_f, g_buf, sem, big_sem, send_sem, recv_sem):
    me = my_index()
    right, left = (me + 1) % NDEV, (me + NDEV - 1) % NDEV
    barrier = pltpu.get_barrier_semaphore()
    for d in (left, right):
        pl.semaphore_signal(barrier, inc=1, device_id=device_of(d), device_id_type=MESH)
    parts = []
    for part, (first, count, ref, at) in enumerate(((0, 2 * HALO, top, HALO), (ROWS - 2 * HALO, 2 * HALO, low, 0), (0, ROWS, mid, 0))):
        parts.append([pltpu.make_async_copy(
            fields_ref.at[pl.ds(first, count), :, pl.ds(b * BW, BW)],
            ref.at[pl.ds(at, count), b], sem.at[part * NB + b]) for b in range(NB)])
    for c in parts[0] + parts[1]:
        c.start()
    load_blend = pltpu.make_async_copy(blend_hbm, blend_v, big_sem.at[0])
    load_blend.start()
    for c in parts[2]:
        c.start()
    load_tab = pltpu.make_async_copy(tab_hbm, tab_v, big_sem.at[1])
    load_tab.start()
    for c in parts[0] + parts[1]:
        c.wait()
    pl.semaphore_wait(barrier, 2)
    halos = []
    for i, (src, dst, d) in enumerate(((low.at[pl.ds(HALO, HALO)], top.at[pl.ds(0, HALO)], right),
                                       (top.at[pl.ds(HALO, HALO)], low.at[pl.ds(2 * HALO, HALO)], left))):
        halos.append(pltpu.make_async_remote_copy(
            src_ref=src, dst_ref=dst, send_sem=send_sem.at[i], recv_sem=recv_sem.at[i],
            device_id=device_of(d), device_id_type=MESH))
    for c in halos:
        c.start()
    load_blend.wait()
    for c in parts[2]:
        c.wait()

    def cycles(first, count, ref):
        blocks = ref.reshape(ref.shape[0] * NB, FL, BW)

        def cycle(r, carry):
            p = local_row(me, r)
            for b in range(NB):
                total = None
                for k in range(K):
                    at = dep_ref[(r * NB + b) * K + k]
                    term = blend_v[r, b, pl.ds(k, 1), :] * blocks[at].astype(F32)
                    total = term if total is None else total + term
                dep_f[b // 2, :, pl.ds((b % 2) * BW, BW)] = total
            rows = pl.ds(pl.multiple_of(p * FL, FL), FL)
            for half in range(2):
                lanes = pl.ds(half * 128, 128)
                g = dft20([dep_f[b, :, lanes] for b in range(20)])
                pairs = [(g[0][0], g[10][0])] + [g[i] for i in range(1, 10)]
                for i, (re, im) in enumerate(pairs):
                    g_buf[i, rows, pl.ds(half * 128, 128)] = re.astype(BF)
                    g_buf[i, rows, pl.ds(256 + half * 128, 128)] = im.astype(BF)
            return carry

        lax.fori_loop(first, first + count, cycle, 0)

    cycles(HALO, ROWS - 2 * HALO, mid)
    for c in halos:
        c.wait()
    cycles(0, HALO, top)
    cycles(ROWS - HALO, HALO, low)
    load_tab.wait()

    def group(g, carry):
        v = jnp.dot(g_buf[g], tab_v[g], preferred_element_type=F32).astype(BF)
        lanes = pl.ds(pl.multiple_of(g * 128, 128), 128)
        out_ref[:, 0, :, lanes] = v[:, :128].reshape(ROWS, FL, 128)
        out_ref[:, 1, :, lanes] = v[:, 128:].reshape(ROWS, FL, 128)
        return carry

    lax.fori_loop(0, NG, group, 0)


def block_swap(x):
    lane = lax.broadcasted_iota(jnp.int32, x[0].shape, 1)
    low64 = lane < 64
    low32 = (lane % 64) < 32
    z = [None] * 4
    for a in range(2):
        lo, hi = x[a], x[a + 2]
        z[a] = jnp.where(low64, lo, pltpu.roll(hi, 64, 1))
        z[a + 2] = jnp.where(low64, pltpu.roll(lo, 64, 1), hi)
    y = [None] * 4
    for a in (0, 2):
        lo, hi = z[a], z[a + 1]
        y[a] = jnp.where(low32, lo, pltpu.roll(hi, 32, 1))
        y[a + 1] = jnp.where(low32, pltpu.roll(lo, 96, 1), hi)
    return y


def partner(i):
    x = lax.axis_index("band")
    st = lax.axis_index("set")
    j = (i * 37) % NDEV
    tx = (x + j // 32) % 4
    ty = (st // 8 + (j // 8) % 4) % 4
    tz = ((st // 2) % 4 + (j // 2) % 4) % 4
    tc = (st % 2 + j % 2) % 2
    return tx, (ty * 4 + tz) * 2 + tc


def lat_kernel(f_ref, wave_v, wave_s, damp_s, fwd_hbm, bwd_hbm, out_ref, st_ref,
               natc, xs, rx, xf, uv, s16, zs, fwd_v, bwd_v, big_sem,
               send1, recv1, send2, recv2, own_sem):
    me = my_index()
    load_fwd = pltpu.make_async_copy(fwd_hbm, fwd_v, big_sem.at[0])
    load_bwd = pltpu.make_async_copy(bwd_hbm, bwd_v, big_sem.at[1])
    load_fwd.start()
    load_bwd.start()
    barrier = pltpu.get_barrier_semaphore()
    nat_columns(wave_v, natc)

    fourier = f_ref[...].reshape(ROWS * 32, MM)
    for i in range(MM // 256):
        for j in range(1 + 26 * i, min(27 + 26 * i, NDEV)):
            pl.semaphore_signal(barrier, inc=1, device_id=partner(j), device_id_type=MESH)
        v = lax.dot_general(one_hot(natc[pl.ds(i * 256, 256), :], 0.0, MM), fourier,
                            (((1,), (1,)), ((), ())), preferred_element_type=F32).astype(BF)
        for t in range(TQ):
            xs[t, pl.ds(i * 128, 128)] = v[:, t * 128:(t + 1) * 128].reshape(128, 2, 128)
    pl.semaphore_wait(barrier, NDEV - 1)

    def to_owner(i):
        tx, ts = partner(i)
        return pltpu.make_async_remote_copy(
            src_ref=xs.at[:, pl.ds((tx * 32 + ts) * 5, 5)], dst_ref=rx.at[place_of(me)],
            send_sem=send1.at[i], recv_sem=recv1.at[i], device_id=(tx, ts), device_id_type=MESH)

    def start(i, c):
        to_owner(i).start()
        return c

    def wait(i, c):
        to_owner(i).wait()
        return c

    lax.fori_loop(1, NDEV, start, 0)
    own = pltpu.make_async_copy(xs.at[:, pl.ds(me * 5, 5)], rx.at[place_of(me)], own_sem.at[0])
    own.start()
    own.wait()
    lax.fori_loop(1, NDEV, wait, 0)

    def widen(i, c):
        rows = pl.ds(pl.multiple_of(i * 400, 400), 400)
        xf[rows, :] = rx[pl.ds(i * 8, 8)].reshape(400, 128).astype(F32)
        return c

    lax.fori_loop(0, 16, widen, 0)

    def fold(i, carry):
        sc, t = i // TQ, i % TQ
        for g in range(3):
            us, vs = [], []
            for m in range(4 * g, 4 * g + 4):
                if m >= OWN:
                    us.append(jnp.zeros((16, 128), F32))
                    vs.append(jnp.zeros((16, 128), F32))
                    continue
                lo = xf[pl.ds(sc * 16 * 50 + t * OWN + m, 16, stride=50), :]
                hi = xf[pl.ds((64 + sc * 16) * 50 + t * OWN + m, 16, stride=50), :]
                us.append(lo + hi)
                vs.append(lo - hi)
            for par, vals in ((0, us), (1, vs)):
                y = block_swap(vals)
                for r in range(4):
                    rows = pl.ds(pl.multiple_of(i * 64 + r * 16, 16), 16)
                    uv[par, rows, pl.ds(g * 128, 128)] = y[r].astype(BF)
        return carry

    lax.fori_loop(0, 20, fold, 0)

    lane = lax.broadcasted_iota(jnp.int32, (1, COLS), 1)
    squared = (lane % FL) < LEV
    damp_row = jnp.zeros((1, COLS), F32)
    for f in range(FL):
        damp_row = jnp.where(lane % FL == f, damp_s[f], damp_row)
    wave_row = jnp.full((1, COLS), MM, jnp.int32)
    for m in range(OWN):
        wave_row = jnp.where(lane // 32 == m, wave_s[me * OWN + m], wave_row)
    load_fwd.wait()

    def analyse(i, carry):
        rows = pl.ds(pl.multiple_of(i * 128, 128), 128)
        for par in range(2):
            v = jnp.dot(fwd_v[par, rows, :], uv[par], preferred_element_type=F32)
            n = 2 * (i * 128 + lax.broadcasted_iota(jnp.int32, (128, COLS), 0)) + par
            nf = n.astype(F32)
            q = nf * (nf + 1.0) * (1.0 / (MM * (MM - 1.0)))
            qp = jnp.where(squared, q * q, q)
            v = v * (1.0 / (1.0 + damp_row * qp))
            v = jnp.where(n >= wave_row, v, 0.0)
            for g in range(3):
                st_ref[pl.ds(g * MM + i * 256 + par, 128, stride=2), :] = v[:, g * 128:(g + 1) * 128]
            s16[par, rows, :] = v.astype(BF)
        return carry

    lax.fori_loop(0, 5, analyse, 0)
    load_bwd.wait()
    turn = me % 4

    my_x, my_y, my_z = me // 32, (me // 8) % 4, (me // 4) % 2

    def to_cycles(place, d):
        return pltpu.make_async_remote_copy(
            src_ref=zs.at[place], dst_ref=out_ref.at[:, pl.ds(me * 5, 5)],
            send_sem=send2.at[place], recv_sem=recv2.at[me], device_id=device_of(d), device_id_type=MESH)

    keep = pltpu.make_async_copy(zs.at[place_of(me)], out_ref.at[:, pl.ds(me * 5, 5)], own_sem.at[1])

    def synth(i, carry):
        c = (i + turn) % 4
        rows = pl.ds(pl.multiple_of(c * 320, 320), 320)
        p = jnp.dot(bwd_v[0, rows, :], s16[0], preferred_element_type=F32)
        q = jnp.dot(bwd_v[1, rows, :], s16[1], preferred_element_type=F32)
        for half, z in ((0, p + q), (1, p - q)):
            first = (half * 64 + c * 16) * 50
            for t in range(TQ):
                for g in range(3):
                    y = block_swap([z[(t * 4 + r) * 16:(t * 4 + r + 1) * 16, g * 128:(g + 1) * 128] for r in range(4)])
                    for m in range(4 * g, min(4 * g + 4, OWN)):
                        xf[pl.ds(first + t * OWN + m, 16, stride=50), :] = y[m - 4 * g]
            zs[pl.ds(half * 64 + c * 16, 16)] = (
                xf[pl.ds(pl.multiple_of(first, 8), 800), :].astype(BF).reshape(16, TQ, 5, 2, 128))

        def send(j, carry):
            k = (j * 11) % 32
            tx, ty, tz = (my_x + k // 8) % 4, (my_y + (k // 2) % 4) % 4, (my_z + k % 2) % 2
            far = tx // 2
            d = tx * 32 + ty * 8 + tz * 4 + c + far * (3 - 2 * c)

            @pl.when(d != me)
            def _():
                to_cycles(place_of(d), d).start()

            @pl.when(d == me)
            def _():
                keep.start()

            return carry

        lax.fori_loop(0, 32, send, 0)
        return carry

    lax.fori_loop(0, 4, synth, 0)
    keep.wait()

    def finish(i, c):
        d = (me + i) % NDEV
        place = place_of(d)
        pltpu.make_async_remote_copy(
            src_ref=zs.at[place], dst_ref=out_ref.at[:, pl.ds(d * 5, 5)],
            send_sem=send2.at[place], recv_sem=recv2.at[d], device_id=device_of(d), device_id_type=MESH).wait()
        return c

    lax.fori_loop(1, NDEV, finish, 0)


def wave_kernel(x_ref, wave_v, st_ref, tab_hbm, out_hbm, spec_hbm,
                natc, hot, zt, zn, h_buf, tab_v, rows_v, spec_v, big_sem, row_sem):
    me = my_index()
    load_tab = pltpu.make_async_copy(tab_hbm, tab_v, big_sem.at[0])
    load_tab.start()
    nat_columns(wave_v, natc)

    def hots(i, c):
        rows = pl.ds(pl.multiple_of(i * 128, 128), 128)
        hot[rows, :] = one_hot(natc[rows, :], 0.0, MM)
        return c

    lax.fori_loop(0, MM // 128, hots, 0)

    def turn(t, carry):
        zt[pl.ds(pl.multiple_of(t * 128, 128), 128), :] = jnp.transpose(x_ref[t])
        return carry

    lax.fori_loop(0, TQ, turn, 0)

    def order(i, carry):
        lanes = pl.ds(pl.multiple_of(i * 256, 256), 256)
        v = jnp.dot(zt[...], hot[:, lanes], preferred_element_type=F32).astype(BF)
        zn[:, :, :, lanes] = v.reshape(ROWS, 2, FL, 256)
        return carry

    lax.fori_loop(0, MM // 256, order, 0)
    load_tab.wait()

    def group(g, carry):
        lanes = pl.ds(pl.multiple_of(g * 128, 128), 128)
        re = zn[:, 0, :, lanes].reshape(ROWS * FL, 128)
        im = zn[:, 1, :, lanes].reshape(ROWS * FL, 128)
        v = jnp.concatenate([re, im], axis=1)
        h_buf[g] = jnp.dot(v, tab_v[g], preferred_element_type=F32)
        return carry

    lax.fori_loop(0, NG, group, 0)

    def put(r):
        return pltpu.make_async_copy(rows_v.at[r], out_hbm.at[r], row_sem.at[r])

    def cycle(r, carry):
        rows = pl.ds(pl.multiple_of(local_row(me, r) * FL, FL), FL)
        for half in range(2):
            re = [h_buf[g, rows, pl.ds(half * 128, 128)] for g in range(NG)]
            im = [h_buf[g, rows, pl.ds(256 + half * 128, 128)] for g in range(NG)]
            c = [(re[0], None)] + [(re[g], im[g]) for g in range(1, NG)] + [(im[0], None)]
            y = idft20(c)
            for b in range(20):
                rows_v[r, :, pl.ds(b * 256 + half * 128, 128)] = y[b].astype(BF)
        put(r).start()
        return carry

    lax.fori_loop(0, ROWS, cycle, 0)

    for g in range(3):
        for nt in range(10):
            tr = jnp.transpose(st_ref[pl.ds(g * MM + nt * 128, 128), :])
            for m in range(4 * g, min(4 * g + 4, OWN)):
                for c in range(2):
                    first = (m - 4 * g) * 32 + c * 16
                    spec_v[m, :, c, pl.ds(nt * 128, 128)] = tr[first:first + 16]
    put_spec = pltpu.make_async_copy(spec_v, spec_hbm, big_sem.at[1])
    put_spec.start()

    def done(r, c):
        put(r).wait()
        return c

    lax.fori_loop(0, ROWS, done, 0)
    put_spec.wait()


ANY = pl.BlockSpec(memory_space=pl.ANY)
VM = pl.BlockSpec(memory_space=pltpu.VMEM)
SM = pl.BlockSpec(memory_space=pltpu.SMEM)
LIMIT = 56 * 2**20


def per_device(fields, depart, blend, wave_owner, damping):
    fwd_lat, bwd_lat = latitude_tables()
    dma = pltpu.SemaphoreType.DMA
    row = wave_owner.reshape(1, MM)
    r = jnp.arange(ROWS, dtype=jnp.int32)
    held = jnp.where(r < HALO, -HALO, jnp.where(r >= ROWS - HALO, ROWS - 2 * HALO, 0))
    places = (depart - ((my_index() * ROWS + held) * NB)[:, None, None]).reshape(-1)
    fourier = pl.pallas_call(
        grid_kernel,
        out_shape=jax.ShapeDtypeStruct((ROWS, 2, FL, MM), BF),
        in_specs=[ANY, SM, ANY, ANY],
        out_specs=VM,
        scratch_shapes=[
            pltpu.VMEM((ROWS, NB, FL, BW), BF),
            pltpu.VMEM((3 * HALO, NB, FL, BW), BF),
            pltpu.VMEM((3 * HALO, NB, FL, BW), BF),
            pltpu.VMEM((ROWS, NB, K, BW), F32),
            pltpu.VMEM((NG, 512, 256), BF),
            pltpu.VMEM((20, FL, 256), F32),
            pltpu.VMEM((NG, ROWS * FL, 512), BF),
            dma((3 * NB,)), dma((2,)), dma((2,)), dma((2,)),
        ],
        compiler_params=pltpu.CompilerParams(vmem_limit_bytes=LIMIT, collective_id=0, has_side_effects=True),
        name="grid_step",
    )(fields, places, blend, jnp.asarray(forward_tables()))
    zonal, st = pl.pallas_call(
        lat_kernel,
        out_shape=(jax.ShapeDtypeStruct((TQ, MM // 2, 2, 128), BF), jax.ShapeDtypeStruct((3 * MM, 128), F32)),
        in_specs=[VM, VM, SM, SM, ANY, ANY],
        out_specs=(ANY, VM),
        scratch_shapes=[
            pltpu.VMEM((MM, 128), F32),
            pltpu.VMEM((TQ, MM // 2, 2, 128), BF),
            pltpu.VMEM((NDEV, TQ, 5, 2, 128), BF),
            pltpu.VMEM((NDEV * 50, 128), F32),
            pltpu.VMEM((2, NLAT // 2, COLS), BF),
            pltpu.VMEM((2, MM // 2, COLS), BF),
            pltpu.VMEM((NDEV, TQ, 5, 2, 128), BF),
            pltpu.VMEM((2, MM // 2, NLAT // 2), BF),
            pltpu.VMEM((2, NLAT // 2, MM // 2), BF),
            dma((2,)), dma((NDEV,)), dma((NDEV,)), dma((NDEV,)), dma((NDEV,)), dma((2,)),
        ],
        compiler_params=pltpu.CompilerParams(vmem_limit_bytes=LIMIT, collective_id=1, has_side_effects=True),
        name="latitude_step",
    )(fourier, row, wave_owner, damping, jnp.asarray(fwd_lat), jnp.asarray(bwd_lat))
    updated, spectra = pl.pallas_call(
        wave_kernel,
        out_shape=(jax.ShapeDtypeStruct((ROWS, FL, NLON), BF), jax.ShapeDtypeStruct((OWN, FL, 2, MM), F32)),
        in_specs=[VM, VM, VM, ANY],
        out_specs=(ANY, ANY),
        scratch_shapes=[
            pltpu.VMEM((MM, 128), F32),
            pltpu.VMEM((MM, MM), BF),
            pltpu.VMEM((ROWS * 32, MM), BF),
            pltpu.VMEM((ROWS, 2, FL, MM), BF),
            pltpu.VMEM((NG, ROWS * FL, 512), F32),
            pltpu.VMEM((NG, 256, 512), BF),
            pltpu.VMEM((ROWS, FL, NLON), BF),
            pltpu.VMEM((OWN, FL, 2, MM), F32),
            dma((2,)), dma((ROWS,)),
        ],
        compiler_params=pltpu.CompilerParams(vmem_limit_bytes=LIMIT),
        name="wave_step",
    )(zonal.reshape(TQ, MM, 128), row, st, jnp.asarray(inverse_tables()))
    return (updated, spectra)


def solution(mesh):
    in_specs = (
        P(("band", "set"), None, None),
        P(("band", "set"), None, None),
        P(("band", "set"), None, None, None),
        P(),
        P(),
    )
    out_specs = (P(("band", "set"), None, None), P(("band", "set"), None, None, None))
    return jax.shard_map(
        per_device, mesh=mesh, in_specs=in_specs, out_specs=out_specs, check_vma=False
    )
```

time: 161 us -> 115 us (0.71)
  Pallas kernels: 143 us -> 111 us
  starting transfers between devices: 6.86 us -> 0 us
  waiting for transfers between devices: 3.8 us -> 0 us
  local copies, waits for them, and re-layouts: 5.89 us -> 2.36 us
    pallas_call x5 -> x3, Pallas kernels: 143 us -> 111 us  [the longest x1 76.4 us: per_device(): pl.pallas_call(lat_kernel, out_shape=(jax.ShapeDtypeStruct((TQ, MM // 2,...]
    ppermute x2 -> x0, starting transfers between devices: 6.86 us -> none  [the longest x1 3.53 us: per_device(): lax.ppermute(fields[ROWS - HALO:], ('band', 'set'), [(i, i + 1) for i in...]
    ppermute x2 -> x0, waiting for transfers between devices: 3.8 us -> none  [the longest x1 2.62 us: per_device(): lax.ppermute(fields[:HALO], ('band', 'set'), [(i + 1, i) for i in range(c...]
    broadcast_in_dim x3 -> x0, local copies, waits for them, and re-layouts: 1.75 us -> none  [the longest x1 1.1 us: per_device(): (grp * 128 + jnp.where(m1 >= 10, 64, 0) + m2).astype(jnp.int32)[:, None]]
  transfers between devices with their start and end apart: 2 -> 0, of which waited for: 2 -> 0; matrix products, arithmetic and copies ran while one was open for 2% -> 0% of each run, Pallas kernels for 0% -> 0%
where the time goes in v2:
time: 115 us; the launch traced here: 114 us
  Pallas kernels  111 us (97%)
  local copies, waits for them, and re-layouts  2.36 us (2%)
    pallas_call x1, Pallas kernels, per_device(): pl.pallas_call(lat_kernel, out_shape=(jax.ShapeDtypeStruct((TQ, MM // 2,...  76.4 us
    pallas_call x1, Pallas kernels, per_device(): pl.pallas_call(grid_kernel, out_shape=jax.ShapeDtypeStruct((ROWS, 2, FL,...  21 us
    pallas_call x1, Pallas kernels, per_device(): pl.pallas_call(wave_kernel, out_shape=(jax.ShapeDtypeStruct((ROWS, FL, NL...  13.2 us

profile of v2, /device:TPU:1, one launch (start us, length us, event | category | flops | bytes accessed | tf_op | source)
XLA Modules:
  0.0 114.4 jit_solution(5287928722555164659)
XLA Ops:
  0.6 1.3 %reshape.24.wave_v = s32[1,1280]{1,0:T(1,128)} reshape(s32[1280]{0:T(1024)} %wave_s.1) | data formatting | bytes 10240 | tf_op jit(solution)/shard_map/reshape | solution.py:552
  1.9 0.9 broadcast_subtract_fusion
  2.8 0.2 copy.11
  3.0 0.8 reshape.23.dep_ref
  3.9 21.0 %grid_step.1.f_ref = bf16[20,2,16,1280]{3,2,1,0:T(8,128)(2,1)} custom-call(bf16[20,16,5120]{2,1,0:T(8,128)(2,1)} %fields_ref.1, s32[3200]{0:T(1024)} %reshape.23.dep_ref, f32[20,40,4,128]{3,2,1,0:T(4,128)} %blend_hbm.1, bf16[10,512,256]{2,1,0:T(8,128)(2,1)} %constant.33.clone.tab_hbm), custom_call_target="tpu_custom_call" | custom-call | tf_op jit(solution)/shard_map/grid_step/pallas_call | solution.py:556
  24.9 76.4 %latitude_step.1 = (bf16[5,640,2,128]{3,2,1,0:T(2,128)(2,1)}, f32[3840,128]{1,0:T(8,128)}) custom-call(bf16[20,2,16,1280]{3,2,1,0:T(8,128)(2,1)} %grid_step.1.f_ref, s32[1,1280]{1,0:T(1,128)} %reshape.24.wave_v, s32[1280]{0:T(1024)} %wave_s.1, f32[16]{0:T(128)} %damp_s.1, bf16[2,640,1280]{2,1,0:T(8,128)(2,1)} %constant.34.clone.fwd_hbm, ...), custom_call_target="tpu_custom_call" | custom-call | tf_op jit(solution)/shard_map/latitude_step/pallas_call | solution.py:574
  101.3 13.2 %wave_step.1 = (bf16[20,16,5120]{2,1,0:T(8,128)(2,1)}, f32[10,16,2,1280]{3,2,1,0:T(2,128)}) custom-call(bf16[5,1280,128]{2,1,0:T(8,128)(2,1)} %bitcast.1, s32[1,1280]{1,0:T(1,128)} %reshape.24.wave_v, f32[3840,128]{1,0:T(8,128)} %get-tuple-element.5.st_ref, bf16[10,256,512]{2,1,0:T(8,128)(2,1)} %constant.36.clone.tab_hbm), custom_call_target="tpu_custom_call" | custom-call | tf_op jit(solution)/shard_map/wave_step/pallas_call | solution.py:594
  (1 shorter events, 0.0 us)

commit v3 on v2

--- a/solution.py
+++ b/solution.py
@@ -193,7 +193,7 @@
     nat = (grp * 128 + jnp.where(m1 >= 10, 64, 0) + m2).astype(F32)
     for i in range(MM // 128):
         out_ref[pl.ds(i * 128, 128), :] = jnp.transpose(
-            jnp.broadcast_to(nat[:, i * 128:(i + 1) * 128], (128, 128)))
+            jnp.broadcast_to(nat[i:i + 1, :], (128, 128)))
 
 
 def one_hot(nat, first, count):
@@ -265,21 +265,29 @@
 
         lax.fori_loop(first, first + count, cycle, 0)
 
+    def groups(spans):
+        def group(g, carry):
+            lanes = pl.ds(pl.multiple_of(g * 128, 128), 128)
+            u = jnp.concatenate([g_buf[g, pl.ds(first * FL, count * FL), :] for first, count in spans], axis=0)
+            v = jnp.dot(u, tab_v[g], preferred_element_type=F32).astype(BF)
+            at = 0
+            for first, count in spans:
+                rows = v[at * FL:(at + count) * FL]
+                out_ref[pl.ds(first, count), 0, :, lanes] = rows[:, :128].reshape(count, FL, 128)
+                out_ref[pl.ds(first, count), 1, :, lanes] = rows[:, 128:].reshape(count, FL, 128)
+                at += count
+            return carry
+
+        lax.fori_loop(0, NG, group, 0)
+
     cycles(HALO, ROWS - 2 * HALO, mid)
+    load_tab.wait()
+    groups(((HALO, ROWS - 2 * HALO),))
     for c in halos:
         c.wait()
     cycles(0, HALO, top)
     cycles(ROWS - HALO, HALO, low)
-    load_tab.wait()
-
-    def group(g, carry):
-        v = jnp.dot(g_buf[g], tab_v[g], preferred_element_type=F32).astype(BF)
-        lanes = pl.ds(pl.multiple_of(g * 128, 128), 128)
-        out_ref[:, 0, :, lanes] = v[:, :128].reshape(ROWS, FL, 128)
-        out_ref[:, 1, :, lanes] = v[:, 128:].reshape(ROWS, FL, 128)
-        return carry
-
-    lax.fori_loop(0, NG, group, 0)
+    groups(((0, HALO), (ROWS - HALO, HALO)))
 
 
 def block_swap(x):
@@ -302,16 +310,17 @@
 def partner(i):
     x = lax.axis_index("band")
     st = lax.axis_index("set")
-    j = (i * 37) % NDEV
-    tx = (x + j // 32) % 4
-    ty = (st // 8 + (j // 8) % 4) % 4
-    tz = ((st // 2) % 4 + (j // 2) % 4) % 4
-    tc = (st % 2 + j % 2) % 2
+    j = (i * 37) % 64
+    dz = j % 4
+    tx = (x + j // 16) % 4
+    ty = (st // 8 + (j // 4) % 4) % 4
+    tz = ((st // 2) % 4 + dz) % 4
+    tc = (st % 2 + dz + i // 64) % 2
     return tx, (ty * 4 + tz) * 2 + tc
 
 
-def lat_kernel(f_ref, wave_v, wave_s, damp_s, fwd_hbm, bwd_hbm, out_ref, st_ref,
-               natc, xs, rx, xf, uv, s16, zs, fwd_v, bwd_v, big_sem,
+def lat_kernel(f_ref, wave_v, wave_s, damp_s, fwd_hbm, bwd_hbm, out_ref, spec_hbm,
+               st_ref, spec_v, natc, xs, rx, xf, uv, s16, zs, fwd_v, bwd_v, big_sem,
                send1, recv1, send2, recv2, own_sem):
     me = my_index()
     load_fwd = pltpu.make_async_copy(fwd_hbm, fwd_v, big_sem.at[0])
@@ -341,25 +350,24 @@
         to_owner(i).start()
         return c
 
-    def wait(i, c):
-        to_owner(i).wait()
+    def arrived(i, c):
+        to_owner(i).wait_recv()
+        return c
+
+    def left(i, c):
+        to_owner(i).wait_send()
         return c
 
     lax.fori_loop(1, NDEV, start, 0)
     own = pltpu.make_async_copy(xs.at[:, pl.ds(me * 5, 5)], rx.at[place_of(me)], own_sem.at[0])
     own.start()
     own.wait()
-    lax.fori_loop(1, NDEV, wait, 0)
-
-    def widen(i, c):
-        rows = pl.ds(pl.multiple_of(i * 400, 400), 400)
-        xf[rows, :] = rx[pl.ds(i * 8, 8)].reshape(400, 128).astype(F32)
-        return c
-
-    lax.fori_loop(0, 16, widen, 0)
-
-    def fold(i, carry):
-        sc, t = i // TQ, i % TQ
+    def widen(sc):
+        for half in range(2):
+            first = half * 64 + sc * 16
+            xf[pl.ds(pl.multiple_of(first * 50, 8), 800), :] = rx[pl.ds(first, 16)].reshape(800, 128).astype(F32)
+
+    def fold(sc, t):
         for g in range(3):
             us, vs = [], []
             for m in range(4 * g, 4 * g + 4):
@@ -374,11 +382,25 @@
             for par, vals in ((0, us), (1, vs)):
                 y = block_swap(vals)
                 for r in range(4):
-                    rows = pl.ds(pl.multiple_of(i * 64 + r * 16, 16), 16)
+                    rows = pl.ds(pl.multiple_of((sc * TQ + t) * 64 + r * 16, 16), 16)
                     uv[par, rows, pl.ds(g * 128, 128)] = y[r].astype(BF)
-        return carry
-
-    lax.fori_loop(0, 20, fold, 0)
+
+    same = ((me // 2) + me) % 2
+    for stage in range(2):
+        lax.fori_loop(max(1, 64 * stage), 64 * stage + 64, arrived, 0)
+        low = (same + stage) % 2
+
+        def chunk(q, carry):
+            sc = low + (q // TQ) * (3 - 2 * low)
+
+            @pl.when(q % TQ == 0)
+            def _():
+                widen(sc)
+
+            fold(sc, q % TQ)
+            return carry
+
+        lax.fori_loop(0, 2 * TQ, chunk, 0)
 
     lane = lax.broadcasted_iota(jnp.int32, (1, COLS), 1)
     squared = (lane % FL) < LEV
@@ -453,7 +475,17 @@
         return carry
 
     lax.fori_loop(0, 4, synth, 0)
+    for g in range(3):
+        for nt in range(10):
+            tr = jnp.transpose(st_ref[pl.ds(g * MM + nt * 128, 128), :])
+            for m in range(4 * g, min(4 * g + 4, OWN)):
+                for c in range(2):
+                    first = (m - 4 * g) * 32 + c * 16
+                    spec_v[m, :, c, pl.ds(nt * 128, 128)] = tr[first:first + 16]
+    put_spec = pltpu.make_async_copy(spec_v, spec_hbm, big_sem.at[0])
+    put_spec.start()
     keep.wait()
+    lax.fori_loop(1, NDEV, left, 0)
 
     def finish(i, c):
         d = (me + i) % NDEV
@@ -464,13 +496,17 @@
         return c
 
     lax.fori_loop(1, NDEV, finish, 0)
-
-
-def wave_kernel(x_ref, wave_v, st_ref, tab_hbm, out_hbm, spec_hbm,
+    put_spec.wait()
+
+
+def wave_kernel(x_ref, wave_v, tab_hbm, spec_in, out_hbm, spec_out,
                 natc, hot, zt, zn, h_buf, tab_v, rows_v, spec_v, big_sem, row_sem):
     me = my_index()
     load_tab = pltpu.make_async_copy(tab_hbm, tab_v, big_sem.at[0])
     load_tab.start()
+    take = pltpu.make_async_copy(spec_in, spec_v, big_sem.at[1])
+    hand_on = pltpu.make_async_copy(spec_v, spec_out, big_sem.at[2])
+    take.start()
     nat_columns(wave_v, natc)
 
     def hots(i, c):
@@ -494,6 +530,8 @@
 
     lax.fori_loop(0, MM // 256, order, 0)
     load_tab.wait()
+    take.wait()
+    hand_on.start()
 
     def group(g, carry):
         lanes = pl.ds(pl.multiple_of(g * 128, 128), 128)
@@ -522,23 +560,12 @@
 
     lax.fori_loop(0, ROWS, cycle, 0)
 
-    for g in range(3):
-        for nt in range(10):
-            tr = jnp.transpose(st_ref[pl.ds(g * MM + nt * 128, 128), :])
-            for m in range(4 * g, min(4 * g + 4, OWN)):
-                for c in range(2):
-                    first = (m - 4 * g) * 32 + c * 16
-                    spec_v[m, :, c, pl.ds(nt * 128, 128)] = tr[first:first + 16]
-    put_spec = pltpu.make_async_copy(spec_v, spec_hbm, big_sem.at[1])
-    put_spec.start()
-
     def done(r, c):
         put(r).wait()
         return c
 
     lax.fori_loop(0, ROWS, done, 0)
-    put_spec.wait()
-
+    hand_on.wait()
 
 ANY = pl.BlockSpec(memory_space=pl.ANY)
 VM = pl.BlockSpec(memory_space=pltpu.VMEM)
@@ -549,7 +576,7 @@
 def per_device(fields, depart, blend, wave_owner, damping):
     fwd_lat, bwd_lat = latitude_tables()
     dma = pltpu.SemaphoreType.DMA
-    row = wave_owner.reshape(1, MM)
+    row = wave_owner.reshape(MM // 128, 128)
     r = jnp.arange(ROWS, dtype=jnp.int32)
     held = jnp.where(r < HALO, -HALO, jnp.where(r >= ROWS - HALO, ROWS - 2 * HALO, 0))
     places = (depart - ((my_index() * ROWS + held) * NB)[:, None, None]).reshape(-1)
@@ -571,12 +598,14 @@
         compiler_params=pltpu.CompilerParams(vmem_limit_bytes=LIMIT, collective_id=0, has_side_effects=True),
         name="grid_step",
     )(fields, places, blend, jnp.asarray(forward_tables()))
-    zonal, st = pl.pallas_call(
+    zonal, spectra = pl.pallas_call(
         lat_kernel,
-        out_shape=(jax.ShapeDtypeStruct((TQ, MM // 2, 2, 128), BF), jax.ShapeDtypeStruct((3 * MM, 128), F32)),
+        out_shape=(jax.ShapeDtypeStruct((TQ, MM // 2, 2, 128), BF), jax.ShapeDtypeStruct((OWN, FL, 2, MM), F32)),
         in_specs=[VM, VM, SM, SM, ANY, ANY],
-        out_specs=(ANY, VM),
+        out_specs=(ANY, ANY),
         scratch_shapes=[
+            pltpu.VMEM((3 * MM, 128), F32),
+            pltpu.VMEM((OWN, FL, 2, MM), F32),
             pltpu.VMEM((MM, 128), F32),
             pltpu.VMEM((TQ, MM // 2, 2, 128), BF),
             pltpu.VMEM((NDEV, TQ, 5, 2, 128), BF),
@@ -594,7 +623,7 @@
     updated, spectra = pl.pallas_call(
         wave_kernel,
         out_shape=(jax.ShapeDtypeStruct((ROWS, FL, NLON), BF), jax.ShapeDtypeStruct((OWN, FL, 2, MM), F32)),
-        in_specs=[VM, VM, VM, ANY],
+        in_specs=[VM, VM, ANY, ANY],
         out_specs=(ANY, ANY),
         scratch_shapes=[
             pltpu.VMEM((MM, 128), F32),
@@ -605,11 +634,11 @@
             pltpu.VMEM((NG, 256, 512), BF),
             pltpu.VMEM((ROWS, FL, NLON), BF),
             pltpu.VMEM((OWN, FL, 2, MM), F32),
-            dma((2,)), dma((ROWS,)),
+            dma((3,)), dma((ROWS,)),
         ],
         compiler_params=pltpu.CompilerParams(vmem_limit_bytes=LIMIT),
         name="wave_step",
-    )(zonal.reshape(TQ, MM, 128), row, st, jnp.asarray(inverse_tables()))
+    )(zonal.reshape(TQ, MM, 128), row, jnp.asarray(inverse_tables()), spectra)
     return (updated, spectra)
 
 

time: 115 us -> 107 us (0.930)
  Pallas kernels: 111 us -> 104 us
  local copies, waits for them, and re-layouts: 2.36 us -> 1.06 us
    pallas_call x1, Pallas kernels: 76.4 us -> 72.6 us  [per_device(): pl.pallas_call(lat_kernel, out_shape=(jax.ShapeDtypeStruct((TQ, MM // 2,...]
    pallas_call x1, Pallas kernels: 13.2 us -> 11.1 us  [per_device(): pl.pallas_call(wave_kernel, out_shape=(jax.ShapeDtypeStruct((ROWS, FL, NL...]
    reshape x1 -> x0, local copies, waits for them, and re-layouts: 1.3 us -> none  [per_device(): row = wave_owner.reshape(1, MM)]
where the time goes in v3:
time: 107 us
  Pallas kernels  104 us (97%)
    pallas_call x1, Pallas kernels, per_device(): pl.pallas_call(lat_kernel, out_shape=(jax.ShapeDtypeStruct((TQ, MM // 2,...  72.6 us
    pallas_call x1, Pallas kernels, per_device(): pl.pallas_call(grid_kernel, out_shape=jax.ShapeDtypeStruct((ROWS, 2, FL,...  20.5 us
    pallas_call x1, Pallas kernels, per_device(): pl.pallas_call(wave_kernel, out_shape=(jax.ShapeDtypeStruct((ROWS, FL, NL...  11.1 us

profile of v3, /device:TPU:1, one launch (start us, length us, event | category | flops | bytes accessed | tf_op | source)
XLA Modules:
  0.0 106.8 jit_solution(10418238368556470707)
XLA Ops:
  0.6 0.9 broadcast_subtract_fusion
  1.5 0.2 copy.11
  1.7 0.8 reshape.23.dep_ref
  2.6 20.5 %grid_step.1.f_ref = bf16[20,2,16,1280]{3,2,1,0:T(8,128)(2,1)} custom-call(bf16[20,16,5120]{2,1,0:T(8,128)(2,1)} %fields_ref.1, s32[3200]{0:T(1024)} %reshape.23.dep_ref, f32[20,40,4,128]{3,2,1,0:T(4,128)} %blend_hbm.1, bf16[10,512,256]{2,1,0:T(8,128)(2,1)} %constant.33.clone.tab_hbm), custom_call_target="tpu_custom_call" | custom-call | tf_op jit(solution)/shard_map/grid_step/pallas_call | solution.py:583
  23.1 72.6 %latitude_step.1 = (bf16[5,640,2,128]{3,2,1,0:T(2,128)(2,1)}, f32[10,16,2,1280]{3,2,1,0:T(2,128)}) custom-call(bf16[20,2,16,1280]{3,2,1,0:T(8,128)(2,1)} %grid_step.1.f_ref, s32[10,128]{1,0:T(8,128)} %bitcast.3, s32[1280]{0:T(1024)} %wave_s.1, f32[16]{0:T(128)} %damp_s.1, bf16[2,640,1280]{2,1,0:T(8,128)(2,1)} %constant.34.clone.fwd_hbm, ...), custom_call_target="tpu_custom_call" | custom-call | tf_op jit(solution)/shard_map/latitude_step/pallas_call | solution.py:601
  95.7 11.1 %wave_step.1 = (bf16[20,16,5120]{2,1,0:T(8,128)(2,1)}, f32[10,16,2,1280]{3,2,1,0:T(2,128)}) custom-call(bf16[5,1280,128]{2,1,0:T(8,128)(2,1)} %bitcast.2, s32[10,128]{1,0:T(8,128)} %bitcast.4, bf16[10,256,512]{2,1,0:T(8,128)(2,1)} %constant.36.clone.tab_hbm, f32[10,16,2,1280]{3,2,1,0:T(2,128)} %get-tuple-element.5.spec_in), custom_call_target="tpu_custom_call" | custom-call | tf_op jit(solution)/shard_map/wave_step/pallas_call | solution.py:623
  (1 shorter events, 0.0 us)

commit v4 on v3

--- a/solution.py
+++ b/solution.py
@@ -310,17 +310,16 @@
 def partner(i):
     x = lax.axis_index("band")
     st = lax.axis_index("set")
-    j = (i * 37) % 64
-    dz = j % 4
-    tx = (x + j // 16) % 4
-    ty = (st // 8 + (j // 4) % 4) % 4
-    tz = ((st // 2) % 4 + dz) % 4
-    tc = (st % 2 + dz + i // 64) % 2
+    q, u = i // 32, (i * 11) % 32
+    tx = (x + u // 8) % 4
+    ty = (st // 8 + (u // 2) % 4) % 4
+    tz = ((st // 2) % 4 + 2 * (u % 2) + q % 2) % 4
+    tc = (st % 2 + (q + 1) // 2) % 2
     return tx, (ty * 4 + tz) * 2 + tc
 
 
 def lat_kernel(f_ref, wave_v, wave_s, damp_s, fwd_hbm, bwd_hbm, out_ref, spec_hbm,
-               st_ref, spec_v, natc, xs, rx, xf, uv, s16, zs, fwd_v, bwd_v, big_sem,
+               st_ref, spec_v, natc, natq, xs, rx, xf, uv, s16, zs, fwd_v, bwd_v, big_sem,
                send1, recv1, send2, recv2, own_sem):
     me = my_index()
     load_fwd = pltpu.make_async_copy(fwd_hbm, fwd_v, big_sem.at[0])
@@ -330,25 +329,21 @@
     barrier = pltpu.get_barrier_semaphore()
     nat_columns(wave_v, natc)
 
+    for j in range(1, NDEV):
+        pl.semaphore_signal(barrier, inc=1, device_id=partner(j), device_id_type=MESH)
+    for q in range(4):
+        for m in range(OWN):
+            natq[pl.ds(q * 320 + m, 32, stride=OWN), :] = natc[pl.ds(q * OWN + m, 32, stride=4 * OWN), :]
     fourier = f_ref[...].reshape(ROWS * 32, MM)
-    for i in range(MM // 256):
-        for j in range(1 + 26 * i, min(27 + 26 * i, NDEV)):
-            pl.semaphore_signal(barrier, inc=1, device_id=partner(j), device_id_type=MESH)
-        v = lax.dot_general(one_hot(natc[pl.ds(i * 256, 256), :], 0.0, MM), fourier,
-                            (((1,), (1,)), ((), ())), preferred_element_type=F32).astype(BF)
-        for t in range(TQ):
-            xs[t, pl.ds(i * 128, 128)] = v[:, t * 128:(t + 1) * 128].reshape(128, 2, 128)
-    pl.semaphore_wait(barrier, NDEV - 1)
+
+    def place_sent(d):
+        return pl.ds(((d % 4) * 32 + d // 4) * 5, 5)
 
     def to_owner(i):
         tx, ts = partner(i)
         return pltpu.make_async_remote_copy(
-            src_ref=xs.at[:, pl.ds((tx * 32 + ts) * 5, 5)], dst_ref=rx.at[place_of(me)],
+            src_ref=xs.at[:, place_sent(tx * 32 + ts)], dst_ref=rx.at[place_of(me)],
             send_sem=send1.at[i], recv_sem=recv1.at[i], device_id=(tx, ts), device_id_type=MESH)
-
-    def start(i, c):
-        to_owner(i).start()
-        return c
 
     def arrived(i, c):
         to_owner(i).wait_recv()
@@ -358,10 +353,21 @@
         to_owner(i).wait_send()
         return c
 
-    lax.fori_loop(1, NDEV, start, 0)
-    own = pltpu.make_async_copy(xs.at[:, pl.ds(me * 5, 5)], rx.at[place_of(me)], own_sem.at[0])
-    own.start()
+    own = pltpu.make_async_copy(xs.at[:, place_sent(me)], rx.at[place_of(me)], own_sem.at[0])
+    low2 = me % 4
+    flip = low2 + 1 - 2 * (low2 % 2)
+    for q, bits in enumerate((low2, 3 - low2, flip, 3 - flip)):
+        v = lax.dot_general(one_hot(natq[pl.ds(pl.multiple_of(bits * 320, 64), 320), :], 0.0, MM), fourier,
+                            (((1,), (1,)), ((), ())), preferred_element_type=F32).astype(BF)
+        for t in range(TQ):
+            xs[t, pl.ds(bits * 160, 160)] = v[:, t * 128:(t + 1) * 128].reshape(160, 2, 128)
+        if q == 0:
+            pl.semaphore_wait(barrier, NDEV - 1)
+            own.start()
+        for i in range(max(1, 32 * q), 32 * q + 32):
+            to_owner(i).start()
     own.wait()
+
     def widen(sc):
         for half in range(2):
             first = half * 64 + sc * 16
@@ -455,23 +461,25 @@
             zs[pl.ds(half * 64 + c * 16, 16)] = (
                 xf[pl.ds(pl.multiple_of(first, 8), 800), :].astype(BF).reshape(16, TQ, 5, 2, 128))
 
-        def send(j, carry):
+        for j in range(32):
             k = (j * 11) % 32
             tx, ty, tz = (my_x + k // 8) % 4, (my_y + (k // 2) % 4) % 4, (my_z + k % 2) % 2
             far = tx // 2
-            d = tx * 32 + ty * 8 + tz * 4 + c + far * (3 - 2 * c)
+            low_bits = c + far * (3 - 2 * c)
+            d = tx * 32 + ty * 8 + tz * 4 + low_bits
+            place = far * 64 + c * 16 + (d // 4 + far * (31 - 2 * (d // 4)))
+            if k > 0:
+                to_cycles(place, d).start()
+                continue
 
             @pl.when(d != me)
             def _():
-                to_cycles(place_of(d), d).start()
+                to_cycles(place, d).start()
 
             @pl.when(d == me)
             def _():
                 keep.start()
 
-            return carry
-
-        lax.fori_loop(0, 32, send, 0)
         return carry
 
     lax.fori_loop(0, 4, synth, 0)
@@ -607,6 +615,7 @@
             pltpu.VMEM((3 * MM, 128), F32),
             pltpu.VMEM((OWN, FL, 2, MM), F32),
             pltpu.VMEM((MM, 128), F32),
+            pltpu.VMEM((MM, 128), F32),
             pltpu.VMEM((TQ, MM // 2, 2, 128), BF),
             pltpu.VMEM((NDEV, TQ, 5, 2, 128), BF),
             pltpu.VMEM((NDEV * 50, 128), F32),

time: 107 us -> 106 us (level)
    pallas_call x1, Pallas kernels: 72.6 us -> 71.2 us  [per_device(): pl.pallas_call(lat_kernel, out_shape=(jax.ShapeDtypeStruct((TQ, MM // 2,...]
where the time goes in v4:
time: 106 us; the launch traced here: 105 us
  Pallas kernels  103 us (97%)
  local copies, waits for them, and re-layouts  1.06 us (1%)
    pallas_call x1, Pallas kernels, per_device(): pl.pallas_call(lat_kernel, out_shape=(jax.ShapeDtypeStruct((TQ, MM // 2,...  71.2 us
    pallas_call x1, Pallas kernels, per_device(): pl.pallas_call(grid_kernel, out_shape=jax.ShapeDtypeStruct((ROWS, 2, FL,...  20.5 us
    pallas_call x1, Pallas kernels, per_device(): pl.pallas_call(wave_kernel, out_shape=(jax.ShapeDtypeStruct((ROWS, FL, NL...  11.1 us

profile of v4, /device:TPU:1, one launch (start us, length us, event | category | flops | bytes accessed | tf_op | source)
XLA Modules:
  0.0 105.4 jit_solution(4856564951490249646)
XLA Ops:
  0.6 0.9 broadcast_subtract_fusion
  1.5 0.2 copy.11
  1.7 0.8 reshape.23.dep_ref
  2.6 20.5 %grid_step.1.f_ref = bf16[20,2,16,1280]{3,2,1,0:T(8,128)(2,1)} custom-call(bf16[20,16,5120]{2,1,0:T(8,128)(2,1)} %fields_ref.1, s32[3200]{0:T(1024)} %reshape.23.dep_ref, f32[20,40,4,128]{3,2,1,0:T(4,128)} %blend_hbm.1, bf16[10,512,256]{2,1,0:T(8,128)(2,1)} %constant.33.clone.tab_hbm), custom_call_target="tpu_custom_call" | custom-call | tf_op jit(solution)/shard_map/grid_step/pallas_call | solution.py:591
  23.1 71.2 %latitude_step.1 = (bf16[5,640,2,128]{3,2,1,0:T(2,128)(2,1)}, f32[10,16,2,1280]{3,2,1,0:T(2,128)}) custom-call(bf16[20,2,16,1280]{3,2,1,0:T(8,128)(2,1)} %grid_step.1.f_ref, s32[10,128]{1,0:T(8,128)} %bitcast.3, s32[1280]{0:T(1024)} %wave_s.1, f32[16]{0:T(128)} %damp_s.1, bf16[2,640,1280]{2,1,0:T(8,128)(2,1)} %constant.34.clone.fwd_hbm, ...), custom_call_target="tpu_custom_call" | custom-call | tf_op jit(solution)/shard_map/latitude_step/pallas_call | solution.py:609
  94.3 11.1 %wave_step.1 = (bf16[20,16,5120]{2,1,0:T(8,128)(2,1)}, f32[10,16,2,1280]{3,2,1,0:T(2,128)}) custom-call(bf16[5,1280,128]{2,1,0:T(8,128)(2,1)} %bitcast.2, s32[10,128]{1,0:T(8,128)} %bitcast.4, bf16[10,256,512]{2,1,0:T(8,128)(2,1)} %constant.36.clone.tab_hbm, f32[10,16,2,1280]{3,2,1,0:T(2,128)} %get-tuple-element.5.spec_in), custom_call_target="tpu_custom_call" | custom-call | tf_op jit(solution)/shard_map/wave_step/pallas_call | solution.py:632
  (1 shorter events, 0.0 us)

commit v5 on v4

--- a/solution.py
+++ b/solution.py
@@ -612,13 +612,13 @@
         in_specs=[VM, VM, SM, SM, ANY, ANY],
         out_specs=(ANY, ANY),
         scratch_shapes=[
-            pltpu.VMEM((3 * MM, 128), F32),
+            pltpu.VMEM((3 * MM + 64, 128), F32),
             pltpu.VMEM((OWN, FL, 2, MM), F32),
-            pltpu.VMEM((MM, 128), F32),
-            pltpu.VMEM((MM, 128), F32),
+            pltpu.VMEM((MM + 64, 128), F32),
+            pltpu.VMEM((MM + 64, 128), F32),
             pltpu.VMEM((TQ, MM // 2, 2, 128), BF),
             pltpu.VMEM((NDEV, TQ, 5, 2, 128), BF),
-            pltpu.VMEM((NDEV * 50, 128), F32),
+            pltpu.VMEM((NDEV * 50 + 64, 128), F32),
             pltpu.VMEM((2, NLAT // 2, COLS), BF),
             pltpu.VMEM((2, MM // 2, COLS), BF),
             pltpu.VMEM((NDEV, TQ, 5, 2, 128), BF),

time: 106 us -> 106 us (level)
  no operation moved by 1% of the time
where the time goes in v5:
time: 106 us; the launch traced here: 105 us
  Pallas kernels  103 us (97%)
  local copies, waits for them, and re-layouts  1.06 us (1%)
    pallas_call x1, Pallas kernels, per_device(): pl.pallas_call(lat_kernel, out_shape=(jax.ShapeDtypeStruct((TQ, MM // 2,...  71.2 us
    pallas_call x1, Pallas kernels, per_device(): pl.pallas_call(grid_kernel, out_shape=jax.ShapeDtypeStruct((ROWS, 2, FL,...  20.5 us
    pallas_call x1, Pallas kernels, per_device(): pl.pallas_call(wave_kernel, out_shape=(jax.ShapeDtypeStruct((ROWS, FL, NL...  11.1 us

profile of v5, /device:TPU:1, one launch (start us, length us, event | category | flops | bytes accessed | tf_op | source)
XLA Modules:
  0.0 105.3 jit_solution(5474294202910951681)
XLA Ops:
  0.6 0.9 broadcast_subtract_fusion
  1.5 0.2 copy.11
  1.7 0.8 reshape.23.dep_ref
  2.6 20.5 %grid_step.1.f_ref = bf16[20,2,16,1280]{3,2,1,0:T(8,128)(2,1)} custom-call(bf16[20,16,5120]{2,1,0:T(8,128)(2,1)} %fields_ref.1, s32[3200]{0:T(1024)} %reshape.23.dep_ref, f32[20,40,4,128]{3,2,1,0:T(4,128)} %blend_hbm.1, bf16[10,512,256]{2,1,0:T(8,128)(2,1)} %constant.33.clone.tab_hbm), custom_call_target="tpu_custom_call" | custom-call | tf_op jit(solution)/shard_map/grid_step/pallas_call | solution.py:591
  23.1 71.2 %latitude_step.1 = (bf16[5,640,2,128]{3,2,1,0:T(2,128)(2,1)}, f32[10,16,2,1280]{3,2,1,0:T(2,128)}) custom-call(bf16[20,2,16,1280]{3,2,1,0:T(8,128)(2,1)} %grid_step.1.f_ref, s32[10,128]{1,0:T(8,128)} %bitcast.3, s32[1280]{0:T(1024)} %wave_s.1, f32[16]{0:T(128)} %damp_s.1, bf16[2,640,1280]{2,1,0:T(8,128)(2,1)} %constant.34.clone.fwd_hbm, ...), custom_call_target="tpu_custom_call" | custom-call | tf_op jit(solution)/shard_map/latitude_step/pallas_call | solution.py:609
  94.3 11.1 %wave_step.1 = (bf16[20,16,5120]{2,1,0:T(8,128)(2,1)}, f32[10,16,2,1280]{3,2,1,0:T(2,128)}) custom-call(bf16[5,1280,128]{2,1,0:T(8,128)(2,1)} %bitcast.2, s32[10,128]{1,0:T(8,128)} %bitcast.4, bf16[10,256,512]{2,1,0:T(8,128)(2,1)} %constant.36.clone.tab_hbm, f32[10,16,2,1280]{3,2,1,0:T(2,128)} %get-tuple-element.5.spec_in), custom_call_target="tpu_custom_call" | custom-call | tf_op jit(solution)/shard_map/wave_step/pallas_call | solution.py:632
  (1 shorter events, 0.0 us)
